TPU v7x, 32 devices: a whole 2x2x4 slice. The times are simulated.
32 devices in a mesh: row: 8 (over y, x, core), col: 4 (over z).
Axes of the slice: x: 2, y: 2, z: 4, core: 2. Of those that a mesh axis runs over, the one named last changes fastest.
Arguments:
- sketch: bfloat16 [32, 64, 4, 3, 128], P('row', 'col'), may hold values from -6 to 6
- snapshots: bfloat16 [32, 64, 4, 3, 512], P('row', 'col'), may hold values from -6 to 6
- start_block: float32 [128, 64], replicated, may hold values from -0.5 to 0.5
Outputs:
- galerkin: float32 [64, 4096], replicated
All inputs are finite; a program needn't handle non-finite values.
Results may differ from a plain program's by a relative error of at most 0.0084.
Values may be sent and summed in bfloat16 or wider, within the bound.
A program may use at most 64 MiB of HBM per device.

v0:
```python
import math

import jax
import jax.numpy as jnp
from jax import lax
from jax.sharding import PartitionSpec as P

ITERS = 4


def padded_2(value, sides, width):
    for axis, dim in sides:
        devices, length = (lax.axis_size(axis), value.shape[dim])
        up = [(i, (i + 1) % devices) for i in range(devices)]
        down = [(j, i) for i, j in up]
        last = lax.slice_in_dim(value, length - width, length, axis=dim)
        initial = lax.slice_in_dim(value, 0, width, axis=dim)
        before = lax.ppermute(last, axis, up)
        after = lax.ppermute(initial, axis, down)
        value = jnp.concatenate([before, value, after], axis=dim)
    return value


def body(sketch, snapshots, start_block):
    highest = lax.Precision.HIGHEST
    rows_x, rows_y, span_cells, comps, sketch_cols = sketch.shape
    snap_count = snapshots.shape[4]
    modes_count = start_block.shape[1]
    flat_sketch = sketch.reshape(rows_x * rows_y * span_cells * comps, sketch_cols)
    flat_snap = snapshots.reshape(rows_x * rows_y * span_cells * comps, snap_count)
    local_coeffs = lax.dot_general(
        flat_sketch, flat_snap, (((0,), (0,)), ((), ())), preferred_element_type=jnp.float32
    )
    coeffs = lax.psum(local_coeffs, ("row", "col"))
    projected = jnp.dot(coeffs.T, start_block, precision=highest)
    y_matrix = jnp.dot(coeffs, projected, precision=highest)
    polar = y_matrix / jnp.sqrt(jnp.sum(y_matrix * y_matrix) + 1e-06)
    for repeat in range(ITERS):
        polar = 1.5 * polar - 0.5 * jnp.dot(
            polar, jnp.dot(polar.T, polar, precision=highest), precision=highest
        )
    basis_bf = polar.astype(jnp.bfloat16)
    mode_values = jnp.dot(flat_sketch, basis_bf, preferred_element_type=jnp.float32).astype(
        jnp.bfloat16
    )
    mode_flat = mode_values.reshape(rows_x, rows_y, span_cells * comps * modes_count)
    padded = padded_2(mode_flat, (("row", 0), ("col", 1)), 1)
    padded_cells = padded.reshape(rows_x + 2, rows_y + 2, span_cells, comps, modes_count).astype(
        jnp.float32
    )
    center = padded_cells[1:-1, 1:-1]
    grad_x = (padded_cells[2:, 1:-1] - padded_cells[:-2, 1:-1]) * 0.5
    grad_y = (padded_cells[1:-1, 2:] - padded_cells[1:-1, :-2]) * 0.5
    grad_z = (jnp.roll(center, -1, axis=2) - jnp.roll(center, 1, axis=2)) * 0.5
    gradients = jnp.stack([grad_x, grad_y, grad_z]).astype(jnp.bfloat16)
    mode_field = mode_values.reshape(rows_x, rows_y, span_cells, comps, modes_count)
    plane_rows = rows_y * span_cells * comps

    def plane_step(plane_at, total):
        phi_plane = lax.dynamic_index_in_dim(mode_field, plane_at, 0, keepdims=False)
        grad_plane = lax.dynamic_index_in_dim(gradients, plane_at, 1, keepdims=False)
        advect = jnp.einsum(
            "yzdi,dyzcj->yzcij", phi_plane, grad_plane, preferred_element_type=jnp.float32
        ).astype(jnp.bfloat16)
        partial_term = lax.dot_general(
            phi_plane.reshape(plane_rows, modes_count),
            advect.reshape(plane_rows, modes_count * modes_count),
            (((0,), (0,)), ((), ())),
            preferred_element_type=jnp.float32,
        )
        return total + partial_term

    total = lax.fori_loop(
        0, rows_x, plane_step, jnp.zeros((modes_count, modes_count * modes_count), jnp.float32)
    )
    summed = lax.psum(total, ("row", "col"))
    cell_count = rows_x * lax.axis_size("row") * rows_y * lax.axis_size("col") * span_cells
    return summed * (1.0 / math.sqrt(cell_count))


def solution(mesh):
    return jax.shard_map(
        body,
        mesh=mesh,
        in_specs=(P("row", "col", None, None, None), P("row", "col", None, None, None), P()),
        out_specs=P(),
        check_vma=False,
    )
```

profile of v0, /device:TPU:0, one launch (start us, length us, event | category | flops | bytes accessed | tf_op | source)
XLA Modules:
  0.0 357.2 jit_solution(11770299746812803023)
XLA Ops:
  6.5 1.1 copy-done
  7.7 1.9 convolution_bitcast_fusion
  10.9 129.6 %all-reduce.3.cloned.1.call-done = f32[128,512]{1,0:T(8,128)} async-done(((f32[128,512]{1,0:T(8,128)}), f32[128,512]{1,0:T(8,128)}) %all-reduce.3.cloned.1.call-update) | async-done | bytes 262160 | tf_op jit(solution)/shard_map/psum | solution.py:34
  140.5 1.5 fusion.20
  142.1 2.2 multiply_reduce_fusion
  147.6 2.7 collective-permute-start.1
  151.9 1.5 collective-permute-start.2
  153.4 2.4 collective-permute-start.3
  158.8 1.6 pad_maximum_fusion
  160.5 56.2 %while.14 = (s32[]{:T(128)}, f32[64,4096]{1,0:T(8,128)S(1)}, bf16[4,16,4,3,64]{4,3,2,1,0:T(4,128)(2,1)}, bf16[3,4,16,4,3,64]{5,4,3,2,1,0:T(4,128)(2,1)}, s32[]{:T(128)}, /*index=5*/s32[]{:T(128)}) while((s32[]{:T(128)}, f32[64,4096]{1,0:T(8,128)S(1)}, bf16[4,16,4,3,64]{4,3,2,1,0:T(4,128)(2,1)}, ...), condition=%wide.region_3.4_spmd.clone, body=%wide.region_2.3_spmd.clone.sunk | while | flops 106692608 | bytes 11903071 | solution.py:73
  162.4 2.7 convert_bitcast_fusion.2
  165.1 4.6 %copy.38 = bf16[16,4,3,64,64]{4,3,2,1,0:T(8,128)(2,1)} copy(bf16[16,4,3,64,64]{3,4,2,1,0:T(8,128)(2,1)} %convert_bitcast_fusion.2) | data formatting | bytes 3145728 | tf_op jit(solution)/shard_map/while/body/eval_jaxpr/convert_element_type | solution.py:64
  169.7 4.3 %reshape.99 = bf16[192,4096]{1,0:T(8,128)(2,1)S(1)} reshape(bf16[16,4,3,64,64]{4,3,2,1,0:T(8,128)(2,1)} %copy.38) | data formatting | bytes 3145728 | tf_op jit(solution)/shard_map/while/body/eval_jaxpr/reshape | solution.py:67
  176.4 2.7 convert_bitcast_fusion.2
  179.1 4.6 %copy.38 = bf16[16,4,3,64,64]{4,3,2,1,0:T(8,128)(2,1)} copy(bf16[16,4,3,64,64]{3,4,2,1,0:T(8,128)(2,1)} %convert_bitcast_fusion.2) | data formatting | bytes 3145728 | tf_op jit(solution)/shard_map/while/body/eval_jaxpr/convert_element_type | solution.py:64
  183.8 4.3 %reshape.99 = bf16[192,4096]{1,0:T(8,128)(2,1)S(1)} reshape(bf16[16,4,3,64,64]{4,3,2,1,0:T(8,128)(2,1)} %copy.38) | data formatting | bytes 3145728 | tf_op jit(solution)/shard_map/while/body/eval_jaxpr/reshape | solution.py:67
  190.5 2.7 convert_bitcast_fusion.2
  193.2 4.6 %copy.38 = bf16[16,4,3,64,64]{4,3,2,1,0:T(8,128)(2,1)} copy(bf16[16,4,3,64,64]{3,4,2,1,0:T(8,128)(2,1)} %convert_bitcast_fusion.2) | data formatting | bytes 3145728 | tf_op jit(solution)/shard_map/while/body/eval_jaxpr/convert_element_type | solution.py:64
  197.8 4.3 %reshape.99 = bf16[192,4096]{1,0:T(8,128)(2,1)S(1)} reshape(bf16[16,4,3,64,64]{4,3,2,1,0:T(8,128)(2,1)} %copy.38) | data formatting | bytes 3145728 | tf_op jit(solution)/shard_map/while/body/eval_jaxpr/reshape | solution.py:67
  204.6 2.7 convert_bitcast_fusion.2
  207.2 4.6 %copy.38 = bf16[16,4,3,64,64]{4,3,2,1,0:T(8,128)(2,1)} copy(bf16[16,4,3,64,64]{3,4,2,1,0:T(8,128)(2,1)} %convert_bitcast_fusion.2) | data formatting | bytes 3145728 | tf_op jit(solution)/shard_map/while/body/eval_jaxpr/convert_element_type | solution.py:64
  211.9 4.3 %reshape.99 = bf16[192,4096]{1,0:T(8,128)(2,1)S(1)} reshape(bf16[16,4,3,64,64]{4,3,2,1,0:T(8,128)(2,1)} %copy.38) | data formatting | bytes 3145728 | tf_op jit(solution)/shard_map/while/body/eval_jaxpr/reshape | solution.py:67
  217.7 130.4 %all-reduce.5.cloned.1.call-done = f32[64,4096]{1,0:T(8,128)} async-done(((f32[64,4096]{1,0:T(8,128)}), f32[64,4096]{1,0:T(8,128)}) %all-reduce.5.cloned.1.call-update) | async-done | bytes 1048592 | tf_op jit(solution)/shard_map/psum | solution.py:76
  348.1 2.3 broadcast_multiply_fusion
  (58 shorter events, 19.2 us)
Async XLA Ops:
  6.5 1.1 copy-start
  6.5 134.0 %all-reduce.3.cloned.1.call-start = ((), (), s32[]{:S(2)}) async-start(), calls=%async_computation | async-start | bytes 524288 | tf_op jit(solution)/shard_map/psum | solution.py:34
  9.6 338.5 %all-reduce.5.cloned.1.call-start = ((), (), s32[]{:S(2)}) async-start(), calls=%async_computation.1 | async-start | bytes 2097152 | tf_op jit(solution)/shard_map/psum | solution.py:76
  147.2 4.2 %collective-permute-start = (bf16[1,16,768]{2,1,0:T(8,128)(2,1)S(1)}, bf16[1,16,768]{2,1,0:T(8,128)(2,1)S(1)}, u32[]{:S(2)}, u32[]{:S(2)}) collective-permute-start(bf16[1,16,768]{2,1,0:T(8,128)(2,1)S(1)} %slice.52), channel_id=1, source_target_pairs={{0,4},{4,8},{8,12},{12,16},{16,20},{20,24},{24,28},{28,0},{1,5},{5... | collective-permute-start | bytes 73736 | tf_op jit(solution)/shard_map/ppermute | solution.py:18
  147.6 4.2 %collective-permute-start.1 = (bf16[1,16,768]{2,1,0:T(8,128)(2,1)S(1)}, bf16[1,16,768]{2,1,0:T(8,128)(2,1)S(1)}, u32[]{:S(2)}, u32[]{:S(2)}) collective-permute-start(bf16[1,16,768]{2,1,0:T(8,128)(2,1)S(1)} %slice.54), channel_id=1, source_target_pairs={{4,0},{8,4},{12,8},{16,12},{20,16},{24,20},{28,24},{0,28},{5,1},{9... | collective-permute-start | bytes 73736 | tf_op jit(solution)/shard_map/ppermute | solution.py:19
  151.9 5.7 %collective-permute-start.2 = (bf16[6,1,768]{2,1,0:T(2,128)(2,1)S(1)}, bf16[6,1,768]{2,1,0:T(2,128)(2,1)S(1)}, u32[]{:S(2)}, u32[]{:S(2)}) collective-permute-start(bf16[6,1,768]{2,1,0:T(2,128)(2,1)S(1)} %get-tuple-element.122), channel_id=1, source_target_pairs={{0,1},{1,2},{2,3},{3,0},{4,5},{5,6},{6,7},{7,4},{8,9},{9,10},{10,1... | collective-permute-start | bytes 27656 | tf_op jit(solution)/shard_map/ppermute | solution.py:18
  153.4 4.2 %collective-permute-start.3 = (bf16[6,1,768]{2,1,0:T(2,128)(2,1)S(1)}, bf16[6,1,768]{2,1,0:T(2,128)(2,1)S(1)}, u32[]{:S(2)}, u32[]{:S(2)}) collective-permute-start(bf16[6,1,768]{2,1,0:T(2,128)(2,1)S(1)} %get-tuple-element.123), channel_id=1, source_target_pairs={{1,0},{2,1},{3,2},{0,3},{5,4},{6,5},{7,6},{4,7},{9,8},{10,9},{11,1... | collective-permute-start | bytes 27656 | tf_op jit(solution)/shard_map/ppermute | solution.py:19
  216.7 1.0 copy-start.1
Sparse Core Ops, SparseCore 0:
  12.9 127.6 all-reduce.2
  217.8 130.2 all-reduce.4
where the time goes:
time: 358 us; the launch traced here: 357 us
  waiting for transfers between devices  262 us (73%)
  local copies, waits for them, and re-layouts  48.9 us (14%)
  matrix products  20.3 us (6%)
  between operations  14.3 us (4%)
  starting transfers between devices  6.68 us (2%)
  other arithmetic  4.48 us (1%)
    psum x1, waiting for transfers between devices, body(): summed = lax.psum(total, ('row', 'col'))  130 us
    psum x1, waiting for transfers between devices, body(): coeffs = lax.psum(local_coeffs, ('row', 'col'))  130 us
    convert_element_type x4, local copies, waits for them, and re-layouts, plane_step(): advect = jnp.einsum('yzdi,dyzcj->yzcij', phi_plane, grad_plane, preferred...  18.6 us
    reshape x4, local copies, waits for them, and re-layouts, plane_step(): advect.reshape(plane_rows, modes_count * modes_count)  17 us
    dot_general x4, matrix products, plane_step(): jnp.einsum('yzdi,dyzcj->yzcij', phi_plane, grad_plane, preferred_element_...  10.7 us
  transfers between devices with their start and end apart: 6, of which 5 were waited for; matrix products, arithmetic and copies ran while one was open for 1% of the time, Pallas kernels for 0%

commit v1 on v0

v1 whole, which is shorter than its diff:
```python
import functools
import math

import jax
import jax.numpy as jnp
import numpy as np
from jax import lax
from jax.experimental import pallas as pl
from jax.experimental.pallas import tpu as pltpu
from jax.sharding import PartitionSpec as P

ITERS = 4
MESH = pl.DeviceIdType.MESH
F32 = jnp.float32
BF16 = jnp.bfloat16
HIGHEST = lax.Precision.HIGHEST
NT = (((1,), (1,)), ((), ()))


def neighbour_columns(nx, ny, nz):
    plane = ny * nz
    cells = nx * plane
    slab = 16
    x, y, z = np.meshgrid(np.arange(nx), np.arange(ny), np.arange(nz), indexing="ij")
    cell = x * plane + y * nz + z
    x_before, x_after = cells, cells + plane
    y_before = cells + 2 * plane
    y_after = y_before + nx * slab
    ahead = [
        np.where(x < nx - 1, cell + plane, x_after + y * nz + z),
        np.where(y < ny - 1, cell + nz, y_after + x * slab + z),
        np.where(z < nz - 1, cell + 1, cell - (nz - 1)),
    ]
    behind = [
        np.where(x > 0, cell - plane, x_before + y * nz + z),
        np.where(y > 0, cell - nz, y_before + x * slab + slab - nz + z),
        np.where(z > 0, cell - 1, cell + nz - 1),
    ]
    both = [np.concatenate([v.reshape(-1) for v in side]) for side in (ahead, behind)]
    return np.stack(both).astype(np.int32)


def kernel(
    chips, cols, scale,
    c_ref, sk_ref, start_ref, near_ref, out_ref,
    hx, hy, rc1, acc1, rc2, rc3, cfull,
    diff, phi, phi_all, grad, adv,
    sg1, rg1, sg2, rg2, sg3, rg3, gfull,
    hs, hr, a1s, a1r, a2s, a2r, a3s, a3r, a4s, a4r, a5s, a5r,
    g1s, g1r, g2s, g2r, g3s, g3r, g4s, g4r, g5s, g5r, g6s, g6r,
):
    rows = 2 * chips
    row, col = lax.axis_index("row"), lax.axis_index("col")
    chip, core = row // 2, lax.rem(row, 2)
    sibling = (row + 1 - 2 * core, col)
    row_up, row_down = lax.rem(row + 1, rows), lax.rem(row + rows - 1, rows)
    col_up, col_down = lax.rem(col + 1, cols), lax.rem(col + cols - 1, cols)
    row_other = lax.rem(row + rows + 2 * core - 1, rows)

    def chip_at(offset):
        return lax.rem(chip + offset, chips)

    def col_at(offset):
        return lax.rem(col + offset, cols)

    def on_chip(q):
        return (2 * q + core, col)

    def push(src, dst, send, recv, device):
        return pltpu.make_async_remote_copy(
            src_ref=src, dst_ref=dst, send_sem=send, recv_sem=recv,
            device_id=device, device_id_type=MESH,
        )

    barrier = pltpu.get_barrier_semaphore()
    partners = [sibling, (row_other, col)]
    partners += [on_chip(chip_at(o)) for o in range(1, chips)]
    partners += [(row, col_at(o)) for o in range(1, cols)]
    for device in partners:
        pl.semaphore_signal(barrier, inc=1, device_id=device, device_id_type=MESH)
    pl.semaphore_wait(barrier, len(partners))

    a1 = push(c_ref.at[1 - core], rc1, a1s.at[0], a1r.at[0], sibling)
    a1.start()
    nx, plane = sk_ref.shape[1:3]
    halos = [
        push(sk_ref.at[:, nx - 1], hx.at[0], hs.at[0], hr.at[0], (row_up, col)),
        push(sk_ref.at[:, 0], hx.at[1], hs.at[1], hr.at[1], (row_down, col)),
        push(sk_ref.at[:, :, pl.ds(plane - 16, 16)], hy.at[0], hs.at[2], hr.at[2], (row, col_up)),
        push(sk_ref.at[:, :, pl.ds(0, 16)], hy.at[1], hs.at[3], hr.at[3], (row, col_down)),
    ]
    for copy in halos:
        copy.start()
    a1.wait_recv()
    acc1[...] = c_ref[core] + rc1[...]
    a2 = []
    for o in range(1, chips):
        q = chip_at(o)
        copy = push(acc1.at[q], rc2.at[chip], a2s.at[o], a2r.at[chip], on_chip(q))
        copy.start()
        a2.append(copy)

    extent, wide = diff.shape
    place = lax.broadcasted_iota(jnp.int32, (extent, wide), 0)
    diff[...] = (
        jnp.where(place == near_ref[0:1, :], 0.5, 0.0)
        - jnp.where(place == near_ref[1:2, :], 0.5, 0.0)
    ).astype(BF16)

    total = acc1[chip]
    for o in range(1, chips):
        q = chip_at(o)
        push(rc2.at[q], rc2.at[q], a2s.at[o], a2r.at[q], sibling).wait_recv()
        total = total + rc2[q]
    rc3[col] = total
    a3 = []
    for o in range(1, cols):
        copy = push(rc3.at[col], rc3.at[col], a3s.at[o], a3r.at[col], (row, col_at(o)))
        copy.start()
        a3.append(copy)
    for o in range(1, cols):
        z = col_at(o)
        push(rc3.at[z], rc3.at[z], a3s.at[o], a3r.at[z], sibling).wait_recv()
    total = rc3[0]
    for z in range(1, cols):
        total = total + rc3[z]
    cfull[core, chip] = total
    own = cfull.at[core, chip]
    a5 = [push(own, own, a5s.at[0], a5r.at[chip], sibling)]
    a4 = []
    for o in range(1, chips):
        copy = push(own, own, a4s.at[o], a4r.at[chip], on_chip(chip_at(o)))
        copy.start()
        a4.append(copy)
    a5[0].start()
    for o in range(1, chips):
        q = chip_at(o)
        block = cfull.at[core, q]
        push(block, block, a4s.at[o], a4r.at[q], sibling).wait_recv()
        copy = push(block, block, a5s.at[o], a5r.at[q], sibling)
        copy.start()
        a5.append(copy)
    for q in range(chips):
        block = cfull.at[1 - core, q]
        push(block, block, a5s.at[0], a5r.at[q], sibling).wait_recv()

    coeffs = cfull[...].reshape(-1, cfull.shape[-1])
    start = start_ref[...].T
    projected = jnp.dot(start, coeffs, precision=HIGHEST, preferred_element_type=F32)
    y_matrix = lax.dot_general(projected, coeffs, NT, precision=HIGHEST, preferred_element_type=F32)
    polar = y_matrix / jnp.sqrt(jnp.sum(y_matrix * y_matrix) + 1e-06)
    for _ in range(ITERS):
        gram = lax.dot_general(polar, polar, NT, precision=HIGHEST, preferred_element_type=F32)
        polar = 1.5 * polar - 0.5 * jnp.dot(
            gram, polar, precision=HIGHEST, preferred_element_type=F32
        )
    basis = polar.astype(BF16)
    modes, rank = basis.shape

    for copy in halos:
        copy.wait_recv()
    cells = nx * plane
    for c in range(3):
        inner = sk_ref[c].reshape(cells, rank)
        outer = jnp.concatenate(
            [hx[0, c], hx[1, c], hy[0, c].reshape(-1, rank), hy[1, c].reshape(-1, rank)], axis=0
        )
        field = lax.dot_general(basis, inner, NT, preferred_element_type=F32).astype(BF16)
        rim = lax.dot_general(basis, outer, NT, preferred_element_type=F32).astype(BF16)
        phi[c] = field.astype(F32).reshape(phi.shape[1:])
        phi_all[:, c * cells:(c + 1) * cells] = field
        slopes = jnp.dot(
            jnp.concatenate([field, rim], axis=1), diff[...], preferred_element_type=F32
        ).astype(BF16).astype(F32)
        for d in range(3):
            grad[d, c] = slopes[:, d * cells:(d + 1) * cells]

    blocks = gfull.shape[2]
    count = 128 * blocks // modes

    def part(which, q):
        group_at = which * chips + q
        for ct in range(cells // 128):
            lanes = slice(ct * 128, ct * 128 + 128)
            for group in range(0, count, 4):
                some = range(group, min(group + 4, count))
                p = [[phi[d, group_at, i:i + 1, lanes] for d in range(3)] for i in some]
                for c in range(3):
                    for jt in range(0, modes, 16):
                        g = [grad[d, c, jt:jt + 16, lanes] for d in range(3)]
                        for i, pi in zip(some, p):
                            adv[
                                i * modes + jt:i * modes + jt + 16,
                                c * cells + ct * 128:c * cells + ct * 128 + 128,
                            ] = (pi[0] * g[0] + pi[1] * g[1] + pi[2] * g[2]).astype(BF16)
        value = lax.dot_general(phi_all[...], adv[...], NT, preferred_element_type=F32)
        return [value[:, n * 128:n * 128 + 128] for n in range(blocks)]

    def theirs(step, carry):
        q = chip_at(step + 1)
        for n, value in enumerate(part(1 - core, q)):
            sg1[q, n] = value.astype(BF16)
        push(sg1.at[q], rg1.at[q], g1s.at[q], g1r.at[q], sibling).start()
        return carry

    lax.fori_loop(0, chips, theirs, 0)

    def ours(q):
        values = part(core, q)
        push(rg1.at[q], rg1.at[q], g1s.at[q], g1r.at[q], sibling).wait_recv()
        return [value + rg1[q, n].astype(F32) for n, value in enumerate(values)]

    def for_others(step, carry):
        q = chip_at(step + 1)
        for n, value in enumerate(ours(q)):
            sg2[q, n] = value.astype(BF16)
        push(sg2.at[q], rg2.at[chip], g2s.at[q], g2r.at[chip], on_chip(q)).start()
        return carry

    lax.fori_loop(0, chips - 1, for_others, 0)
    sums = ours(chip)
    for o in range(1, chips):
        q = chip_at(o)
        push(rg2.at[q], rg2.at[q], g2s.at[q], g2r.at[q], sibling).wait_recv()
        sums = [value + rg2[q, n].astype(F32) for n, value in enumerate(sums)]

    share = blocks // cols
    later = []
    if share:
        for n, value in enumerate(sums):
            sg3[n // share, n % share] = value.astype(BF16)
        for o in range(1, cols):
            z = col_at(o)
            copy = push(sg3.at[z], rg3.at[col], g3s.at[z], g3r.at[col], (row, z))
            copy.start()
            later.append(copy)
        final = sg3[col].astype(F32)
        for o in range(1, cols):
            z = col_at(o)
            push(rg3.at[z], rg3.at[z], g3s.at[z], g3r.at[z], sibling).wait_recv()
            final = final + rg3[z].astype(F32)
        own = gfull.at[core, chip, pl.ds(col * share, share)]
        own[...] = final.astype(BF16)
        for o in range(1, cols):
            z = col_at(o)
            copy = push(own, own, g4s.at[z], g4r.at[col], (row, z))
            copy.start()
            later.append(copy)
        for o in range(1, cols):
            z = col_at(o)
            block = gfull.at[core, chip, pl.ds(z * share, share)]
            push(block, block, g4s.at[z], g4r.at[z], sibling).wait_recv()
    else:
        for n, value in enumerate(sums):
            rg3[col, n] = value.astype(BF16)
        for o in range(1, cols):
            z = col_at(o)
            copy = push(rg3.at[col], rg3.at[col], g3s.at[z], g3r.at[col], (row, z))
            copy.start()
            later.append(copy)
        for o in range(1, cols):
            z = col_at(o)
            push(rg3.at[z], rg3.at[z], g3s.at[z], g3r.at[z], sibling).wait_recv()
        final = rg3[0].astype(F32)
        for z in range(1, cols):
            final = final + rg3[z].astype(F32)
        gfull[core, chip] = final.astype(BF16)

    own = gfull.at[core, chip]
    for o in range(1, chips):
        q = chip_at(o)
        copy = push(own, own, g5s.at[q], g5r.at[chip], on_chip(q))
        copy.start()
        later.append(copy)
    copy = push(own, own, g6s.at[chip], g6r.at[chip], sibling)
    copy.start()
    later.append(copy)

    def write(which, q):
        for n in range(blocks):
            at = pl.multiple_of(((which * chips + q) * blocks + n) * 128, 128)
            out_ref[:, pl.ds(at, 128)] = gfull[which, q, n].astype(F32) * scale

    write(core, chip)
    for o in range(1, chips):
        q = chip_at(o)
        block = gfull.at[core, q]
        push(block, block, g5s.at[q], g5r.at[q], sibling).wait_recv()
        copy = push(block, block, g6s.at[q], g6r.at[q], sibling)
        copy.start()
        later.append(copy)
        write(core, q)
    for o in range(chips):
        q = chip_at(o)
        block = gfull.at[1 - core, q]
        push(block, block, g6s.at[q], g6r.at[q], sibling).wait_recv()
        write(1 - core, q)

    for copy in [a1, *halos, *a2, *a3, *a4, *a5, *later]:
        copy.wait_send()
    for q in range(chips):
        push(sg1.at[q], rg1.at[q], g1s.at[q], g1r.at[q], sibling).wait_send()
    for o in range(1, chips):
        q = chip_at(o)
        push(sg2.at[q], rg2.at[q], g2s.at[q], g2r.at[q], sibling).wait_send()


def body(chips, cols, sketch, snapshots, start_block):
    nx, ny, nz, comps, rank = sketch.shape
    snaps = snapshots.shape[-1]
    modes = start_block.shape[1]
    cells = nx * ny * nz
    coeffs = lax.dot_general(
        sketch.reshape(cells * comps, rank), snapshots.reshape(cells * comps, snaps),
        (((0,), (0,)), ((), ())), preferred_element_type=F32,
    )
    depth = rank // (2 * chips)
    coeffs = coeffs.reshape(2, chips, depth, snaps)
    by_comp = sketch.transpose(3, 0, 1, 2, 4).reshape(comps, nx, ny * nz, rank)
    near = jnp.asarray(neighbour_columns(nx, ny, nz))
    extent = cells + 2 * ny * nz + 2 * nx * 16
    blocks = modes * modes // (2 * chips * 128)
    share = max(blocks // cols, 1)
    scale = 1.0 / math.sqrt(cells * 2 * chips * cols)
    counts = [4, 4, 1, 1] + [chips] * 2 + [cols] * 2 + [chips] * 4
    counts += [chips] * 4 + [cols] * 4 + [chips] * 4
    vmem = pl.BlockSpec(memory_space=pltpu.VMEM)
    return pl.pallas_call(
        functools.partial(kernel, chips, cols, scale),
        out_shape=jax.ShapeDtypeStruct((modes, modes * modes), F32),
        in_specs=[vmem] * 4,
        out_specs=vmem,
        scratch_shapes=[
            pltpu.VMEM((2, comps, ny * nz, rank), BF16),
            pltpu.VMEM((2, comps, nx, 16, rank), BF16),
            pltpu.VMEM((chips, depth, snaps), F32),
            pltpu.VMEM((chips, depth, snaps), F32),
            pltpu.VMEM((chips, depth, snaps), F32),
            pltpu.VMEM((cols, depth, snaps), F32),
            pltpu.VMEM((2, chips, depth, snaps), F32),
            pltpu.VMEM((extent, 3 * cells), BF16),
            pltpu.VMEM((comps, 2 * chips, modes // (2 * chips), cells), F32),
            pltpu.VMEM((modes, comps * cells), BF16),
            pltpu.VMEM((3, comps, modes, cells), F32),
            pltpu.VMEM((blocks * 128, comps * cells), BF16),
            pltpu.VMEM((chips, blocks, modes, 128), BF16),
            pltpu.VMEM((chips, blocks, modes, 128), BF16),
            pltpu.VMEM((chips, blocks, modes, 128), BF16),
            pltpu.VMEM((chips, blocks, modes, 128), BF16),
            pltpu.VMEM((cols, share, modes, 128), BF16),
            pltpu.VMEM((cols, share, modes, 128), BF16),
            pltpu.VMEM((2, chips, blocks, modes, 128), BF16),
        ] + [pltpu.SemaphoreType.DMA((n,)) for n in counts],
        compiler_params=pltpu.CompilerParams(
            collective_id=0, has_side_effects=True, vmem_limit_bytes=40 * 1024 * 1024
        ),
    )(coeffs, by_comp, start_block, near)


def solution(mesh):
    chips, cols = mesh.shape["row"] // 2, mesh.shape["col"]
    return jax.shard_map(
        functools.partial(body, chips, cols),
        mesh=mesh,
        in_specs=(P("row", "col", None, None, None), P("row", "col", None, None, None), P()),
        out_specs=P(),
        check_vma=False,
    )
```

time: 358 us -> 49.7 us (0.14)
  waiting for transfers between devices: 262 us -> 0 us
  Pallas kernels: 0 us -> 43.6 us
  local copies, waits for them, and re-layouts: 48.9 us -> 5.45 us
  matrix products: 20.3 us -> 0.26 us
  between operations: 14.3 us -> 0.07 us
  starting transfers between devices: 6.68 us -> 0 us
  other arithmetic: 4.48 us -> 0 us
    psum x2 -> x0, waiting for transfers between devices: 260 us -> none  [the longest x1 130 us: body(): summed = lax.psum(total, ('row', 'col'))]
    pallas_call x0 -> x1, Pallas kernels: none -> 43.6 us  [body(): pl.pallas_call(functools.partial(kernel, chips, cols, scale), out_shape=j...]
    dot_general x20 -> x1, matrix products: 20.3 us -> 0.26 us  [body(): lax.dot_general(sketch.reshape(cells * comps, rank), snapshots.reshape(ce...]
    convert_element_type x6 -> x0, local copies, waits for them, and re-layouts: 19.2 us -> none  [the longest x4 18.6 us: plane_step(): advect = jnp.einsum('yzdi,dyzcj->yzcij', phi_plane, grad_plane, preferred...]
    reshape x11 -> x2, local copies, waits for them, and re-layouts: 18.3 us -> 0.85 us  [the longest x1 0.7 us: body(): snapshots.reshape(cells * comps, snaps)]
    dynamic_slice x8 -> x0, local copies, waits for them, and re-layouts: 7.49 us -> none  [the longest x4 4.03 us: plane_step(): lax.dynamic_index_in_dim(gradients, plane_at, 1, keepdims=False)]
    ppermute x4 -> x0, starting transfers between devices: 6.64 us -> none  [the longest x2 5.1 us: padded_2(): after = lax.ppermute(initial, axis, down)]
  transfers between devices with their start and end apart: 6 -> 0, of which waited for: 5 -> 0; matrix products, arithmetic and copies ran while one was open for 1% -> 0% of each run, Pallas kernels for 0% -> 0%
where the time goes in v1:
time: 49.7 us; the launch traced here: 49.4 us
  Pallas kernels  43.6 us (88%)
  local copies, waits for them, and re-layouts  5.45 us (11%)
    pallas_call x1, Pallas kernels, body(): pl.pallas_call(functools.partial(kernel, chips, cols, scale), out_shape=j...  43.6 us
    unnamed x10, local copies, waits for them, and re-layouts  4.37 us

profile of v1, /device:TPU:0, one launch (start us, length us, event | category | flops | bytes accessed | tf_op | source)
XLA Modules:
  0.0 49.4 jit_solution(8690863753990862018)
XLA Ops:
  0.0 1.7 %copy.14 = bf16[4,16,4,3,512]{4,3,2,1,0:T(4,128)(2,1)S(1)} copy(bf16[4,16,4,3,512]{4,2,3,1,0:T(4,128)(2,1)} %param.5) | data formatting | bytes 1572864 | tf_op args[1]
  1.7 0.0 copy-start.1
  1.7 0.7 %reshape.14 = bf16[768,512,1,1]{1,0,2,3:T(8,128)(2,1)S(1)} reshape(bf16[4,16,4,3,512]{4,3,2,1,0:T(4,128)(2,1)S(1)} %copy.14) | data formatting | bytes 1572864 | tf_op jit(solution)/shard_map/reshape | solution.py:314
  2.5 0.2 copy-done.1
  2.7 0.1 copy.12
  2.8 0.2 reshape.11
  2.9 0.1 copy.13
  3.1 0.3 fusion.c_ref
  3.4 0.0 copy-start.2
  3.4 0.1 copy.15
  3.5 0.7 %copy-done.2 = f32[128,64]{0,1:T(8,128)S(1)} copy-done((f32[128,64]{0,1:T(8,128)S(1)}, f32[128,64]{0,1:T(8,128)}, u32[]{:S(2)}) %copy-start.2) | copy-done | bytes 32792
  4.1 0.0 copy-start
  4.1 0.1 copy.16.start_ref
  4.2 0.6 %copy-done = s32[2,768]{1,0:T(2,128)S(1)} copy-done((s32[2,768]{1,0:T(2,128)S(1)}, s32[2,768]{1,0:T(2,128)}, u32[]{:S(2)}) %copy-start) | copy-done | bytes 6168
  4.8 43.6 %shard_map.46 = f32[64,4096]{1,0:T(8,128)S(1)} custom-call(f32[2,4,16,512]{3,2,1,0:T(8,128)S(1)} %fusion.c_ref, bf16[3,4,64,128]{3,2,1,0:T(8,128)(2,1)S(1)} %bitcast.8, f32[128,64]{1,0:T(8,128)S(1)} %copy.16.start_ref, s32[2,768]{1,0:T(2,128)S(1)} %copy-done), custom_call_target="tpu_custom_call" | custom-call | tf_op jit(solution)/shard_map/pallas_call | solution.py:328
  48.4 1.0 %copy.19 = f32[64,4096]{1,0:T(8,128)} copy(f32[64,4096]{1,0:T(8,128)S(1)} %shard_map.46) | data formatting | bytes 2097152
Async XLA Ops:
  1.7 0.9 %copy-start.1 = (bf16[4,16,4,3,128]{4,2,3,1,0:T(4,128)(2,1)S(1)}, bf16[4,16,4,3,128]{4,2,3,1,0:T(4,128)(2,1)}, u32[]{:S(2)}) copy-start(bf16[4,16,4,3,128]{4,2,3,1,0:T(4,128)(2,1)} %param.4) | copy-start | bytes 589828
  3.4 0.8 %copy-start.2 = (f32[128,64]{0,1:T(8,128)S(1)}, f32[128,64]{0,1:T(8,128)}, u32[]{:S(2)}) copy-start(f32[128,64]{0,1:T(8,128)} %param.6) | copy-start | bytes 98308
  4.1 0.7 %copy-start = (s32[2,768]{1,0:T(2,128)S(1)}, s32[2,768]{1,0:T(2,128)}, u32[]{:S(2)}) copy-start(s32[2,768]{1,0:T(2,128)} %constant.2.clone.near_ref) | copy-start | bytes 18436

commit v2 on v1

--- a/solution.py
+++ b/solution.py
@@ -3,7 +3,6 @@
 
 import jax
 import jax.numpy as jnp
-import numpy as np
 from jax import lax
 from jax.experimental import pallas as pl
 from jax.experimental.pallas import tpu as pltpu
@@ -21,29 +20,28 @@
     plane = ny * nz
     cells = nx * plane
     slab = 16
-    x, y, z = np.meshgrid(np.arange(nx), np.arange(ny), np.arange(nz), indexing="ij")
-    cell = x * plane + y * nz + z
+    cell = lax.broadcasted_iota(jnp.int32, (1, cells), 1)
+    x, y, z = cell // plane, lax.rem(cell // nz, ny), lax.rem(cell, nz)
     x_before, x_after = cells, cells + plane
     y_before = cells + 2 * plane
     y_after = y_before + nx * slab
     ahead = [
-        np.where(x < nx - 1, cell + plane, x_after + y * nz + z),
-        np.where(y < ny - 1, cell + nz, y_after + x * slab + z),
-        np.where(z < nz - 1, cell + 1, cell - (nz - 1)),
+        jnp.where(x < nx - 1, cell + plane, x_after + y * nz + z),
+        jnp.where(y < ny - 1, cell + nz, y_after + x * slab + z),
+        jnp.where(z < nz - 1, cell + 1, cell - (nz - 1)),
     ]
     behind = [
-        np.where(x > 0, cell - plane, x_before + y * nz + z),
-        np.where(y > 0, cell - nz, y_before + x * slab + slab - nz + z),
-        np.where(z > 0, cell - 1, cell + nz - 1),
+        jnp.where(x > 0, cell - plane, x_before + y * nz + z),
+        jnp.where(y > 0, cell - nz, y_before + x * slab + slab - nz + z),
+        jnp.where(z > 0, cell - 1, cell + nz - 1),
     ]
-    both = [np.concatenate([v.reshape(-1) for v in side]) for side in (ahead, behind)]
-    return np.stack(both).astype(np.int32)
+    return ahead, behind
 
 
 def kernel(
-    chips, cols, scale,
-    c_ref, sk_ref, start_ref, near_ref, out_ref,
-    hx, hy, rc1, acc1, rc2, rc3, cfull,
+    chips, cols, span, scale,
+    flat_ref, snap_ref, sk_ref, start_ref, out_ref,
+    sk_cols, hx, hy, sc1, rc1, acc1, rc2, rc3, cfull,
     diff, phi, phi_all, grad, adv,
     sg1, rg1, sg2, rg2, sg3, rg3, gfull,
     hs, hr, a1s, a1r, a2s, a2r, a3s, a3r, a4s, a4r, a5s, a5r,
@@ -78,9 +76,16 @@
     partners += [(row, col_at(o)) for o in range(1, cols)]
     for device in partners:
         pl.semaphore_signal(barrier, inc=1, device_id=device, device_id_type=MESH)
+
+    sk_cols[...] = flat_ref[...].T.reshape(sk_cols.shape)
+
+    def projection(which):
+        half = jnp.dot(sk_cols[which], snap_ref[...], preferred_element_type=F32)
+        return half.reshape(sc1.shape)
+
+    sc1[...] = projection(1 - core)
     pl.semaphore_wait(barrier, len(partners))
-
-    a1 = push(c_ref.at[1 - core], rc1, a1s.at[0], a1r.at[0], sibling)
+    a1 = push(sc1, rc1, a1s.at[0], a1r.at[0], sibling)
     a1.start()
     nx, plane = sk_ref.shape[1:3]
     halos = [
@@ -91,8 +96,9 @@
     ]
     for copy in halos:
         copy.start()
+    mine = projection(core)
     a1.wait_recv()
-    acc1[...] = c_ref[core] + rc1[...]
+    acc1[...] = mine + rc1[...]
     a2 = []
     for o in range(1, chips):
         q = chip_at(o)
@@ -100,12 +106,13 @@
         copy.start()
         a2.append(copy)
 
-    extent, wide = diff.shape
-    place = lax.broadcasted_iota(jnp.int32, (extent, wide), 0)
-    diff[...] = (
-        jnp.where(place == near_ref[0:1, :], 0.5, 0.0)
-        - jnp.where(place == near_ref[1:2, :], 0.5, 0.0)
-    ).astype(BF16)
+    extent = diff.shape[0]
+    cells = nx * plane
+    place = lax.broadcasted_iota(jnp.int32, (extent, cells), 0)
+    for d, (fore, aft) in enumerate(zip(*neighbour_columns(nx, plane // span, span))):
+        diff[:, d * cells:(d + 1) * cells] = (
+            jnp.where(place == fore, 0.5, 0.0) - jnp.where(place == aft, 0.5, 0.0)
+        ).astype(BF16)
 
     total = acc1[chip]
     for o in range(1, chips):
@@ -145,7 +152,7 @@
         push(block, block, a5s.at[0], a5r.at[q], sibling).wait_recv()
 
     coeffs = cfull[...].reshape(-1, cfull.shape[-1])
-    start = start_ref[...].T
+    start = start_ref[...]
     projected = jnp.dot(start, coeffs, precision=HIGHEST, preferred_element_type=F32)
     y_matrix = lax.dot_general(projected, coeffs, NT, precision=HIGHEST, preferred_element_type=F32)
     polar = y_matrix / jnp.sqrt(jnp.sum(y_matrix * y_matrix) + 1e-06)
@@ -159,7 +166,6 @@
 
     for copy in halos:
         copy.wait_recv()
-    cells = nx * plane
     for c in range(3):
         inner = sk_ref[c].reshape(cells, rank)
         outer = jnp.concatenate(
@@ -239,17 +245,13 @@
             z = col_at(o)
             push(rg3.at[z], rg3.at[z], g3s.at[z], g3r.at[z], sibling).wait_recv()
             final = final + rg3[z].astype(F32)
+        gfull[core, chip, pl.ds(col * share, share)] = final.astype(BF16)
         own = gfull.at[core, chip, pl.ds(col * share, share)]
-        own[...] = final.astype(BF16)
         for o in range(1, cols):
             z = col_at(o)
             copy = push(own, own, g4s.at[z], g4r.at[col], (row, z))
             copy.start()
             later.append(copy)
-        for o in range(1, cols):
-            z = col_at(o)
-            block = gfull.at[core, chip, pl.ds(z * share, share)]
-            push(block, block, g4s.at[z], g4r.at[z], sibling).wait_recv()
     else:
         for n, value in enumerate(sums):
             rg3[col, n] = value.astype(BF16)
@@ -266,35 +268,52 @@
             final = final + rg3[z].astype(F32)
         gfull[core, chip] = final.astype(BF16)
 
-    own = gfull.at[core, chip]
-    for o in range(1, chips):
-        q = chip_at(o)
-        copy = push(own, own, g5s.at[q], g5r.at[chip], on_chip(q))
+    pieces = cols if share else 1
+    width = blocks // pieces
+
+    def piece(which, q, z):
+        return gfull.at[which, q, pl.ds(z * width, width)]
+
+    def write(which, q, z):
+        for n in range(width):
+            block = z * width + n
+            at = pl.multiple_of(((which * chips + q) * blocks + block) * 128, 128)
+            out_ref[:, pl.ds(at, 128)] = gfull[which, q, block].astype(F32) * scale
+
+    def forward(q, z):
+        part_of = piece(core, q, z)
+        copy = push(part_of, part_of, g6s.at[q * pieces + z], g6r.at[q * pieces + z], sibling)
         copy.start()
         later.append(copy)
-    copy = push(own, own, g6s.at[chip], g6r.at[chip], sibling)
-    copy.start()
-    later.append(copy)
-
-    def write(which, q):
-        for n in range(blocks):
-            at = pl.multiple_of(((which * chips + q) * blocks + n) * 128, 128)
-            out_ref[:, pl.ds(at, 128)] = gfull[which, q, n].astype(F32) * scale
-
-    write(core, chip)
-    for o in range(1, chips):
-        q = chip_at(o)
-        block = gfull.at[core, q]
-        push(block, block, g5s.at[q], g5r.at[q], sibling).wait_recv()
-        copy = push(block, block, g6s.at[q], g6r.at[q], sibling)
-        copy.start()
-        later.append(copy)
-        write(core, q)
-    for o in range(chips):
-        q = chip_at(o)
-        block = gfull.at[1 - core, q]
-        push(block, block, g6s.at[q], g6r.at[q], sibling).wait_recv()
-        write(1 - core, q)
+        write(core, q, z)
+
+    order = [col_at(o) for o in range(pieces)] if share else [0]
+    for o, z in enumerate(order):
+        own = piece(core, chip, z)
+        if o:
+            push(own, own, g4s.at[z], g4r.at[z], sibling).wait_recv()
+        for offset in range(1, chips):
+            q = chip_at(offset)
+            copy = push(
+                own, own, g5s.at[q * pieces + z], g5r.at[chip * pieces + z], on_chip(q)
+            )
+            copy.start()
+            later.append(copy)
+        forward(chip, z)
+    for z in order:
+        for offset in range(1, chips):
+            q = chip_at(offset)
+            block = piece(core, q, z)
+            slot = q * pieces + z
+            push(block, block, g5s.at[slot], g5r.at[slot], sibling).wait_recv()
+            forward(q, z)
+    for z in order:
+        for offset in range(chips):
+            q = chip_at(offset)
+            block = piece(1 - core, q, z)
+            slot = q * pieces + z
+            push(block, block, g6s.at[slot], g6r.at[slot], sibling).wait_recv()
+            write(1 - core, q, z)
 
     for copy in [a1, *halos, *a2, *a3, *a4, *a5, *later]:
         copy.wait_send()
@@ -310,29 +329,28 @@
     snaps = snapshots.shape[-1]
     modes = start_block.shape[1]
     cells = nx * ny * nz
-    coeffs = lax.dot_general(
-        sketch.reshape(cells * comps, rank), snapshots.reshape(cells * comps, snaps),
-        (((0,), (0,)), ((), ())), preferred_element_type=F32,
-    )
     depth = rank // (2 * chips)
-    coeffs = coeffs.reshape(2, chips, depth, snaps)
+    flat = sketch.transpose(0, 1, 3, 2, 4).reshape(cells * comps, rank)
+    snap = snapshots.transpose(0, 1, 3, 2, 4).reshape(cells * comps, snaps)
     by_comp = sketch.transpose(3, 0, 1, 2, 4).reshape(comps, nx, ny * nz, rank)
-    near = jnp.asarray(neighbour_columns(nx, ny, nz))
     extent = cells + 2 * ny * nz + 2 * nx * 16
     blocks = modes * modes // (2 * chips * 128)
     share = max(blocks // cols, 1)
     scale = 1.0 / math.sqrt(cells * 2 * chips * cols)
     counts = [4, 4, 1, 1] + [chips] * 2 + [cols] * 2 + [chips] * 4
-    counts += [chips] * 4 + [cols] * 4 + [chips] * 4
+    pieces = cols if blocks // cols else 1
+    counts += [chips] * 4 + [cols] * 4 + [chips * pieces] * 4
     vmem = pl.BlockSpec(memory_space=pltpu.VMEM)
     return pl.pallas_call(
-        functools.partial(kernel, chips, cols, scale),
+        functools.partial(kernel, chips, cols, nz, scale),
         out_shape=jax.ShapeDtypeStruct((modes, modes * modes), F32),
         in_specs=[vmem] * 4,
         out_specs=vmem,
         scratch_shapes=[
+            pltpu.VMEM((2, rank // 2, comps * cells), BF16),
             pltpu.VMEM((2, comps, ny * nz, rank), BF16),
             pltpu.VMEM((2, comps, nx, 16, rank), BF16),
+            pltpu.VMEM((chips, depth, snaps), F32),
             pltpu.VMEM((chips, depth, snaps), F32),
             pltpu.VMEM((chips, depth, snaps), F32),
             pltpu.VMEM((chips, depth, snaps), F32),
@@ -354,7 +372,7 @@
         compiler_params=pltpu.CompilerParams(
             collective_id=0, has_side_effects=True, vmem_limit_bytes=40 * 1024 * 1024
         ),
-    )(coeffs, by_comp, start_block, near)
+    )(flat, snap, by_comp, start_block.T)
 
 
 def solution(mesh):

time: 49.7 us -> 47 us (0.946)
  local copies, waits for them, and re-layouts: 5.45 us -> 3.6 us
    unnamed x10 -> x5, local copies, waits for them, and re-layouts: 4.37 us -> 0.99 us
    transpose x1, local copies, waits for them, and re-layouts: 0.08 us -> 1 us  [body(): by_comp = sketch.transpose(3, 0, 1, 2, 4).reshape(comps, nx, ny * nz, rank)]
    reshape x2 -> x1, local copies, waits for them, and re-layouts: 0.85 us -> 1.61 us  [body(): snap = snapshots.transpose(0, 1, 3, 2, 4).reshape(cells * comps, snaps)]
where the time goes in v2:
time: 47 us; the launch traced here: 46.9 us
  Pallas kernels  43.2 us (92%)
  local copies, waits for them, and re-layouts  3.6 us (8%)
    pallas_call x1, Pallas kernels, body(): pl.pallas_call(functools.partial(kernel, chips, cols, nz, scale), out_sha...  43.2 us
    reshape x1, local copies, waits for them, and re-layouts, body(): snap = snapshots.transpose(0, 1, 3, 2, 4).reshape(cells * comps, snaps)  1.61 us
    transpose x1, local copies, waits for them, and re-layouts, body(): by_comp = sketch.transpose(3, 0, 1, 2, 4).reshape(comps, nx, ny * nz, rank)  1 us
    unnamed x5, local copies, waits for them, and re-layouts  0.99 us

profile of v2, /device:TPU:0, one launch (start us, length us, event | category | flops | bytes accessed | tf_op | source)
XLA Modules:
  0.0 46.9 jit_solution(11388344451018866717)
XLA Ops:
  0.0 1.0 %copy.4 = bf16[3,4,16,4,128]{4,3,2,1,0:T(4,128)(2,1)S(1)} copy(bf16[3,4,16,4,128]{4,3,0,2,1:T(4,128)(2,1)} %bitcast.7) | data formatting | bytes 393216 | tf_op jit(solution)/shard_map/transpose | solution.py:335
  1.0 0.0 copy-start
  1.0 0.0 copy-start.1
  1.0 1.6 %reshape.10.snap_ref = bf16[768,512]{1,0:T(8,128)(2,1)S(1)} reshape(bf16[4,16,3,4,512]{4,3,2,1,0:T(4,128)(2,1)} %bitcast.11) | data formatting | bytes 1572864 | tf_op jit(solution)/shard_map/reshape | solution.py:334
  2.7 0.0 copy-done
  2.7 0.0 copy-done.1
  2.7 43.2 %shard_map.37 = f32[64,4096]{1,0:T(8,128)S(1)} custom-call(bf16[768,128]{1,0:T(8,128)(2,1)S(1)} %bitcast.8, bf16[768,512]{1,0:T(8,128)(2,1)S(1)} %reshape.10.snap_ref, bf16[3,4,64,128]{3,2,1,0:T(8,128)(2,1)S(1)} %bitcast.9, f32[64,128]{1,0:T(8,128)S(1)} %bitcast.10), custom_call_target="tpu_custom_call" | custom-call | tf_op jit(solution)/shard_map/pallas_call | solution.py:344
  45.9 1.0 %copy.6 = f32[64,4096]{1,0:T(8,128)} copy(f32[64,4096]{1,0:T(8,128)S(1)} %shard_map.37) | data formatting | bytes 2097152
Async XLA Ops:
  1.0 1.6 %copy-start = (bf16[4,16,4,3,128]{4,2,3,1,0:T(4,128)(2,1)S(1)}, bf16[4,16,4,3,128]{4,2,3,1,0:T(4,128)(2,1)}, u32[]{:S(2)}) copy-start(bf16[4,16,4,3,128]{4,2,3,1,0:T(4,128)(2,1)} %param.3) | copy-start | bytes 589828
  1.0 1.6 %copy-start.1 = (f32[128,64]{0,1:T(8,128)S(1)}, f32[128,64]{0,1:T(8,128)}, u32[]{:S(2)}) copy-start(f32[128,64]{0,1:T(8,128)} %param.5) | copy-start | bytes 98308

commit v3 on v2

--- a/solution.py
+++ b/solution.py
@@ -12,7 +12,6 @@
 MESH = pl.DeviceIdType.MESH
 F32 = jnp.float32
 BF16 = jnp.bfloat16
-HIGHEST = lax.Precision.HIGHEST
 NT = (((1,), (1,)), ((), ()))
 
 
@@ -38,6 +37,16 @@
     return ahead, behind
 
 
+def halves(value):
+    high = value.astype(BF16)
+    return high, (value - high.astype(F32)).astype(BF16)
+
+
+def wide_left(value):
+    high, low = halves(value)
+    return jnp.concatenate([high, high, low], axis=1)
+
+
 def kernel(
     chips, cols, span, scale,
     flat_ref, snap_ref, sk_ref, start_ref, out_ref,
@@ -153,16 +162,34 @@
 
     coeffs = cfull[...].reshape(-1, cfull.shape[-1])
     start = start_ref[...]
-    projected = jnp.dot(start, coeffs, precision=HIGHEST, preferred_element_type=F32)
-    y_matrix = lax.dot_general(projected, coeffs, NT, precision=HIGHEST, preferred_element_type=F32)
+    modes, rank = start.shape
+    coeffs_h, coeffs_l = halves(coeffs)
+    projected = jnp.dot(
+        wide_left(start),
+        jnp.concatenate([coeffs_h, coeffs_l, coeffs_h], axis=0),
+        preferred_element_type=F32,
+    )
+    y_matrix = lax.dot_general(
+        wide_left(projected),
+        jnp.concatenate([coeffs_h, coeffs_l, coeffs_h], axis=1),
+        NT, preferred_element_type=F32,
+    )
     polar = y_matrix / jnp.sqrt(jnp.sum(y_matrix * y_matrix) + 1e-06)
+    polar = jnp.concatenate([polar, jnp.zeros((-modes % 128, rank), F32)], axis=0)
     for _ in range(ITERS):
-        gram = lax.dot_general(polar, polar, NT, precision=HIGHEST, preferred_element_type=F32)
+        high, low = halves(polar)
+        gram = lax.dot_general(
+            jnp.concatenate([high, high, low], axis=1),
+            jnp.concatenate([high, low, high], axis=1),
+            NT, preferred_element_type=F32,
+        )
         polar = 1.5 * polar - 0.5 * jnp.dot(
-            gram, polar, precision=HIGHEST, preferred_element_type=F32
+            wide_left(gram),
+            jnp.concatenate([high, low, high], axis=0),
+            preferred_element_type=F32,
         )
+    polar = polar[:modes]
     basis = polar.astype(BF16)
-    modes, rank = basis.shape
 
     for copy in halos:
         copy.wait_recv()
@@ -177,7 +204,7 @@
         phi_all[:, c * cells:(c + 1) * cells] = field
         slopes = jnp.dot(
             jnp.concatenate([field, rim], axis=1), diff[...], preferred_element_type=F32
-        ).astype(BF16).astype(F32)
+        ).astype(BF16)
         for d in range(3):
             grad[d, c] = slopes[:, d * cells:(d + 1) * cells]
 
@@ -190,7 +217,13 @@
             lanes = slice(ct * 128, ct * 128 + 128)
             for group in range(0, count, 4):
                 some = range(group, min(group + 4, count))
-                p = [[phi[d, group_at, i:i + 1, lanes] for d in range(3)] for i in some]
+                p = [
+                    [
+                        jnp.broadcast_to(phi[d, group_at, i:i + 1, lanes], (16, 128)).astype(BF16)
+                        for d in range(3)
+                    ]
+                    for i in some
+                ]
                 for c in range(3):
                     for jt in range(0, modes, 16):
                         g = [grad[d, c, jt:jt + 16, lanes] for d in range(3)]
@@ -198,7 +231,7 @@
                             adv[
                                 i * modes + jt:i * modes + jt + 16,
                                 c * cells + ct * 128:c * cells + ct * 128 + 128,
-                            ] = (pi[0] * g[0] + pi[1] * g[1] + pi[2] * g[2]).astype(BF16)
+                            ] = pi[0] * g[0] + pi[1] * g[1] + pi[2] * g[2]
         value = lax.dot_general(phi_all[...], adv[...], NT, preferred_element_type=F32)
         return [value[:, n * 128:n * 128 + 128] for n in range(blocks)]
 
@@ -359,7 +392,7 @@
             pltpu.VMEM((extent, 3 * cells), BF16),
             pltpu.VMEM((comps, 2 * chips, modes // (2 * chips), cells), F32),
             pltpu.VMEM((modes, comps * cells), BF16),
-            pltpu.VMEM((3, comps, modes, cells), F32),
+            pltpu.VMEM((3, comps, modes, cells), BF16),
             pltpu.VMEM((blocks * 128, comps * cells), BF16),
             pltpu.VMEM((chips, blocks, modes, 128), BF16),
             pltpu.VMEM((chips, blocks, modes, 128), BF16),

time: 47 us -> 45.8 us (0.974)
  Pallas kernels: 43.2 us -> 42 us
    pallas_call x1, Pallas kernels: 43.2 us -> 42 us  [body(): pl.pallas_call(functools.partial(kernel, chips, cols, nz, scale), out_sha...]
where the time goes in v3:
time: 45.8 us; the launch traced here: 45.7 us
  Pallas kernels  42 us (92%)
  local copies, waits for them, and re-layouts  3.6 us (8%)
    pallas_call x1, Pallas kernels, body(): pl.pallas_call(functools.partial(kernel, chips, cols, nz, scale), out_sha...  42 us
    reshape x1, local copies, waits for them, and re-layouts, body(): snap = snapshots.transpose(0, 1, 3, 2, 4).reshape(cells * comps, snaps)  1.61 us
    transpose x1, local copies, waits for them, and re-layouts, body(): by_comp = sketch.transpose(3, 0, 1, 2, 4).reshape(comps, nx, ny * nz, rank)  1 us
    unnamed x5, local copies, waits for them, and re-layouts  0.99 us

profile of v3, /device:TPU:0, one launch (start us, length us, event | category | flops | bytes accessed | tf_op | source)
XLA Modules:
  0.0 45.7 jit_solution(7857416747767827753)
XLA Ops:
  0.0 1.0 %copy.4 = bf16[3,4,16,4,128]{4,3,2,1,0:T(4,128)(2,1)S(1)} copy(bf16[3,4,16,4,128]{4,3,0,2,1:T(4,128)(2,1)} %bitcast.7) | data formatting | bytes 393216 | tf_op jit(solution)/shard_map/transpose | solution.py:368
  1.0 0.0 copy-start
  1.0 0.0 copy-start.1
  1.0 1.6 %reshape.10.snap_ref = bf16[768,512]{1,0:T(8,128)(2,1)S(1)} reshape(bf16[4,16,3,4,512]{4,3,2,1,0:T(4,128)(2,1)} %bitcast.11) | data formatting | bytes 1572864 | tf_op jit(solution)/shard_map/reshape | solution.py:367
  2.7 0.0 copy-done
  2.7 0.0 copy-done.1
  2.7 42.0 %shard_map.37 = f32[64,4096]{1,0:T(8,128)S(1)} custom-call(bf16[768,128]{1,0:T(8,128)(2,1)S(1)} %bitcast.8, bf16[768,512]{1,0:T(8,128)(2,1)S(1)} %reshape.10.snap_ref, bf16[3,4,64,128]{3,2,1,0:T(8,128)(2,1)S(1)} %bitcast.9, f32[64,128]{1,0:T(8,128)S(1)} %bitcast.10), custom_call_target="tpu_custom_call" | custom-call | tf_op jit(solution)/shard_map/pallas_call | solution.py:377
  44.7 1.0 %copy.6 = f32[64,4096]{1,0:T(8,128)} copy(f32[64,4096]{1,0:T(8,128)S(1)} %shard_map.37) | data formatting | bytes 2097152
Async XLA Ops:
  1.0 1.6 %copy-start = (bf16[4,16,4,3,128]{4,2,3,1,0:T(4,128)(2,1)S(1)}, bf16[4,16,4,3,128]{4,2,3,1,0:T(4,128)(2,1)}, u32[]{:S(2)}) copy-start(bf16[4,16,4,3,128]{4,2,3,1,0:T(4,128)(2,1)} %param.3) | copy-start | bytes 589828
  1.0 1.6 %copy-start.1 = (f32[128,64]{0,1:T(8,128)S(1)}, f32[128,64]{0,1:T(8,128)}, u32[]{:S(2)}) copy-start(f32[128,64]{0,1:T(8,128)} %param.5) | copy-start | bytes 98308

commit v4 on v3

--- a/solution.py
+++ b/solution.py
@@ -49,8 +49,8 @@
 
 def kernel(
     chips, cols, span, scale,
-    flat_ref, snap_ref, sk_ref, start_ref, out_ref,
-    sk_cols, hx, hy, sc1, rc1, acc1, rc2, rc3, cfull,
+    lie_hbm, snap_hbm, start_hbm, out_ref,
+    lie_ref, snap_ref, start_ref, loads, sk_ref, sk_cols, hx, hy, sc1, rc1, acc1, rc2, rc3, cfull,
     diff, phi, phi_all, grad, adv,
     sg1, rg1, sg2, rg2, sg3, rg3, gfull,
     hs, hr, a1s, a1r, a2s, a2r, a3s, a3r, a4s, a4r, a5s, a5r,
@@ -79,6 +79,14 @@
             device_id=device, device_id_type=MESH,
         )
 
+    fetches = [
+        pltpu.make_async_copy(src, dst, loads.at[n])
+        for n, (src, dst) in enumerate(
+            [(snap_hbm, snap_ref), (lie_hbm, lie_ref), (start_hbm, start_ref)]
+        )
+    ]
+    for copy in fetches:
+        copy.start()
     barrier = pltpu.get_barrier_semaphore()
     partners = [sibling, (row_other, col)]
     partners += [on_chip(chip_at(o)) for o in range(1, chips)]
@@ -86,10 +94,16 @@
     for device in partners:
         pl.semaphore_signal(barrier, inc=1, device_id=device, device_id_type=MESH)
 
-    sk_cols[...] = flat_ref[...].T.reshape(sk_cols.shape)
+    comps, rank = sk_ref.shape[0], sk_ref.shape[-1]
+    for copy in fetches:
+        copy.wait()
+    snaps = snap_ref[...].reshape(-1, snap_ref.shape[-1])
+    sk_cols[...] = lie_ref[...].reshape(-1, rank).T.reshape(sk_cols.shape)
+    for c in range(comps):
+        sk_ref[c] = lie_ref[:, c].reshape(sk_ref.shape[1:])
 
     def projection(which):
-        half = jnp.dot(sk_cols[which], snap_ref[...], preferred_element_type=F32)
+        half = jnp.dot(sk_cols[which], snaps, preferred_element_type=F32)
         return half.reshape(sc1.shape)
 
     sc1[...] = projection(1 - core)
@@ -363,9 +377,8 @@
     modes = start_block.shape[1]
     cells = nx * ny * nz
     depth = rank // (2 * chips)
-    flat = sketch.transpose(0, 1, 3, 2, 4).reshape(cells * comps, rank)
-    snap = snapshots.transpose(0, 1, 3, 2, 4).reshape(cells * comps, snaps)
-    by_comp = sketch.transpose(3, 0, 1, 2, 4).reshape(comps, nx, ny * nz, rank)
+    lie = sketch.transpose(0, 1, 3, 2, 4).reshape(nx * ny, comps, nz, rank)
+    snap = snapshots.transpose(0, 1, 3, 2, 4).reshape(nx * ny * comps, nz, snaps)
     extent = cells + 2 * ny * nz + 2 * nx * 16
     blocks = modes * modes // (2 * chips * 128)
     share = max(blocks // cols, 1)
@@ -377,9 +390,14 @@
     return pl.pallas_call(
         functools.partial(kernel, chips, cols, nz, scale),
         out_shape=jax.ShapeDtypeStruct((modes, modes * modes), F32),
-        in_specs=[vmem] * 4,
+        in_specs=[pl.BlockSpec(memory_space=pltpu.HBM)] * 3,
         out_specs=vmem,
         scratch_shapes=[
+            pltpu.VMEM(lie.shape, BF16),
+            pltpu.VMEM(snap.shape, BF16),
+            pltpu.VMEM((modes, rank), F32),
+            pltpu.SemaphoreType.DMA((3,)),
+            pltpu.VMEM((comps, nx, ny * nz, rank), BF16),
             pltpu.VMEM((2, rank // 2, comps * cells), BF16),
             pltpu.VMEM((2, comps, ny * nz, rank), BF16),
             pltpu.VMEM((2, comps, nx, 16, rank), BF16),
@@ -405,7 +423,7 @@
         compiler_params=pltpu.CompilerParams(
             collective_id=0, has_side_effects=True, vmem_limit_bytes=40 * 1024 * 1024
         ),
-    )(flat, snap, by_comp, start_block.T)
+    )(lie, snap, start_block.T)
 
 
 def solution(mesh):

time: 45.8 us -> 46.4 us (1.013)
    unnamed x5 -> x7, local copies, waits for them, and re-layouts: 0.99 us -> 3.79 us
    reshape x1 -> x0, local copies, waits for them, and re-layouts: 1.61 us -> none  [body(): snap = snapshots.transpose(0, 1, 3, 2, 4).reshape(cells * comps, snaps)]
    transpose x1 -> x0, local copies, waits for them, and re-layouts: 1 us -> none  [body(): by_comp = sketch.transpose(3, 0, 1, 2, 4).reshape(comps, nx, ny * nz, rank)]
where the time goes in v4:
time: 46.4 us; the launch traced here: 46.2 us
  Pallas kernels  42.4 us (91%)
  local copies, waits for them, and re-layouts  3.79 us (8%)
    pallas_call x1, Pallas kernels, body(): pl.pallas_call(functools.partial(kernel, chips, cols, nz, scale), out_sha...  42.4 us
    unnamed x7, local copies, waits for them, and re-layouts  3.79 us

profile of v4, /device:TPU:0, one launch (start us, length us, event | category | flops | bytes accessed | tf_op | source)
XLA Modules:
  0.0 46.2 jit_solution(3234106110779604552)
XLA Ops:
  0.0 0.0 copy-start
  0.0 1.1 %copy-done = bf16[4,16,4,3,512]{4,2,3,1,0:T(4,128)(2,1)S(1)} copy-done((bf16[4,16,4,3,512]{4,2,3,1,0:T(4,128)(2,1)S(1)}, bf16[4,16,4,3,512]{4,2,3,1,0:T(4,128)(2,1)}, u32[]{:S(2)}) %copy-start) | copy-done | bytes 786456
  1.1 0.0 copy-start.1
  1.1 0.9 %copy-done.1 = bf16[4,16,4,3,128]{4,2,3,1,0:T(4,128)(2,1)S(1)} copy-done((bf16[4,16,4,3,128]{4,2,3,1,0:T(4,128)(2,1)S(1)}, bf16[4,16,4,3,128]{4,2,3,1,0:T(4,128)(2,1)}, u32[]{:S(2)}) %copy-start.1) | copy-done | bytes 196632
  2.1 0.0 copy-start.2
  2.1 0.8 %copy-done.2 = f32[128,64]{0,1:T(8,128)S(1)} copy-done((f32[128,64]{0,1:T(8,128)S(1)}, f32[128,64]{0,1:T(8,128)}, u32[]{:S(2)}) %copy-start.2) | copy-done | bytes 32792
  2.8 42.4 %shard_map.37 = f32[64,4096]{1,0:T(8,128)S(1)} custom-call(bf16[64,3,4,128]{3,2,1,0:T(4,128)(2,1)S(1)} %bitcast.8, bf16[192,4,512]{2,1,0:T(4,128)(2,1)S(1)} %bitcast.7, f32[64,128]{1,0:T(8,128)S(1)} %bitcast.9), custom_call_target="tpu_custom_call" | custom-call | tf_op jit(solution)/shard_map/pallas_call | solution.py:390
  45.2 1.0 %copy.5 = f32[64,4096]{1,0:T(8,128)} copy(f32[64,4096]{1,0:T(8,128)S(1)} %shard_map.37) | data formatting | bytes 2097152
Async XLA Ops:
  0.0 1.1 %copy-start = (bf16[4,16,4,3,512]{4,2,3,1,0:T(4,128)(2,1)S(1)}, bf16[4,16,4,3,512]{4,2,3,1,0:T(4,128)(2,1)}, u32[]{:S(2)}) copy-start(bf16[4,16,4,3,512]{4,2,3,1,0:T(4,128)(2,1)} %param.4) | copy-start | bytes 2359300
  1.1 0.9 %copy-start.1 = (bf16[4,16,4,3,128]{4,2,3,1,0:T(4,128)(2,1)S(1)}, bf16[4,16,4,3,128]{4,2,3,1,0:T(4,128)(2,1)}, u32[]{:S(2)}) copy-start(bf16[4,16,4,3,128]{4,2,3,1,0:T(4,128)(2,1)} %param.3) | copy-start | bytes 589828
  2.1 0.8 %copy-start.2 = (f32[128,64]{0,1:T(8,128)S(1)}, f32[128,64]{0,1:T(8,128)}, u32[]{:S(2)}) copy-start(f32[128,64]{0,1:T(8,128)} %param.5) | copy-start | bytes 98308

commit v5 on v4

--- a/solution.py
+++ b/solution.py
@@ -421,7 +421,7 @@
             pltpu.VMEM((2, chips, blocks, modes, 128), BF16),
         ] + [pltpu.SemaphoreType.DMA((n,)) for n in counts],
         compiler_params=pltpu.CompilerParams(
-            collective_id=0, has_side_effects=True, vmem_limit_bytes=40 * 1024 * 1024
+            collective_id=0, has_side_effects=True, vmem_limit_bytes=60 * 1024 * 1024
         ),
     )(lie, snap, start_block.T)
 

time: 46.4 us -> 45.4 us (0.978)
  local copies, waits for them, and re-layouts: 3.79 us -> 2.27 us
  Pallas kernels: 42.4 us -> 43 us
    unnamed x7 -> x1, local copies, waits for them, and re-layouts: 3.79 us -> 2.27 us
    pallas_call x1, Pallas kernels: 42.4 us -> 43 us  [body(): pl.pallas_call(functools.partial(kernel, chips, cols, nz, scale), out_sha...]
where the time goes in v5:
time: 45.4 us; the launch traced here: 45.3 us
  Pallas kernels  43 us (95%)
  local copies, waits for them, and re-layouts  2.27 us (5%)
    pallas_call x1, Pallas kernels, body(): pl.pallas_call(functools.partial(kernel, chips, cols, nz, scale), out_sha...  43 us
    unnamed x1, local copies, waits for them, and re-layouts  2.27 us

profile of v5, /device:TPU:0, one launch (start us, length us, event | category | flops | bytes accessed | tf_op | source)
XLA Modules:
  0.0 45.3 jit_solution(8106592386097597090)
XLA Ops:
  0.0 43.0 %shard_map.37 = f32[64,4096]{1,0:T(8,128)} custom-call(bf16[64,3,4,128]{3,2,1,0:T(4,128)(2,1)} %bitcast.8, bf16[192,4,512]{2,1,0:T(4,128)(2,1)} %bitcast.7, f32[64,128]{1,0:T(8,128)} %bitcast.9), custom_call_target="tpu_custom_call" | custom-call | tf_op jit(solution)/shard_map/pallas_call | solution.py:390
  43.0 2.3 %copy.5 = f32[64,4096]{1,0:T(8,128)} copy(f32[64,4096]{1,0:T(8,128)} %shard_map.37) | data formatting | bytes 2097152

commit v6 on v5

--- a/solution.py
+++ b/solution.py
@@ -48,9 +48,9 @@
 
 
 def kernel(
-    chips, cols, span, scale,
+    chips, cols, span,
     lie_hbm, snap_hbm, start_hbm, out_ref,
-    lie_ref, snap_ref, start_ref, loads, sk_ref, sk_cols, hx, hy, sc1, rc1, acc1, rc2, rc3, cfull,
+    lie_ref, snap_ref, start_ref, loads, stores, sk_ref, sk_cols, hx, hy, sc1, rc1, acc1, rc2, rc3, cfull,
     diff, phi, phi_all, grad, adv,
     sg1, rg1, sg2, rg2, sg3, rg3, gfull,
     hs, hr, a1s, a1r, a2s, a2r, a3s, a3r, a4s, a4r, a5s, a5r,
@@ -215,7 +215,9 @@
         field = lax.dot_general(basis, inner, NT, preferred_element_type=F32).astype(BF16)
         rim = lax.dot_general(basis, outer, NT, preferred_element_type=F32).astype(BF16)
         phi[c] = field.astype(F32).reshape(phi.shape[1:])
-        phi_all[:, c * cells:(c + 1) * cells] = field
+        phi_all[c * cells:(c + 1) * cells] = lax.dot_general(
+            inner, basis, NT, preferred_element_type=F32
+        ).astype(BF16)
         slopes = jnp.dot(
             jnp.concatenate([field, rim], axis=1), diff[...], preferred_element_type=F32
         ).astype(BF16)
@@ -246,8 +248,8 @@
                                 i * modes + jt:i * modes + jt + 16,
                                 c * cells + ct * 128:c * cells + ct * 128 + 128,
                             ] = pi[0] * g[0] + pi[1] * g[1] + pi[2] * g[2]
-        value = lax.dot_general(phi_all[...], adv[...], NT, preferred_element_type=F32)
-        return [value[:, n * 128:n * 128 + 128] for n in range(blocks)]
+        value = jnp.dot(adv[...], phi_all[...], preferred_element_type=F32)
+        return [value[n * 128:n * 128 + 128].T for n in range(blocks)]
 
     def theirs(step, carry):
         q = chip_at(step + 1)
@@ -321,11 +323,15 @@
     def piece(which, q, z):
         return gfull.at[which, q, pl.ds(z * width, width)]
 
+    outs = []
+
     def write(which, q, z):
-        for n in range(width):
-            block = z * width + n
-            at = pl.multiple_of(((which * chips + q) * blocks + block) * 128, 128)
-            out_ref[:, pl.ds(at, 128)] = gfull[which, q, block].astype(F32) * scale
+        slot = (which * chips + q) * pieces + z
+        copy = pltpu.make_async_copy(
+            piece(which, q, z), out_ref.at[pl.ds(slot * width, width)], stores.at[slot]
+        )
+        copy.start()
+        outs.append(copy)
 
     def forward(q, z):
         part_of = piece(core, q, z)
@@ -362,6 +368,8 @@
             push(block, block, g6s.at[slot], g6r.at[slot], sibling).wait_recv()
             write(1 - core, q, z)
 
+    for copy in outs:
+        copy.wait()
     for copy in [a1, *halos, *a2, *a3, *a4, *a5, *later]:
         copy.wait_send()
     for q in range(chips):
@@ -386,17 +394,17 @@
     counts = [4, 4, 1, 1] + [chips] * 2 + [cols] * 2 + [chips] * 4
     pieces = cols if blocks // cols else 1
     counts += [chips] * 4 + [cols] * 4 + [chips * pieces] * 4
-    vmem = pl.BlockSpec(memory_space=pltpu.VMEM)
-    return pl.pallas_call(
-        functools.partial(kernel, chips, cols, nz, scale),
-        out_shape=jax.ShapeDtypeStruct((modes, modes * modes), F32),
+    tensor = pl.pallas_call(
+        functools.partial(kernel, chips, cols, nz),
+        out_shape=jax.ShapeDtypeStruct((2 * chips * blocks, modes, 128), BF16),
         in_specs=[pl.BlockSpec(memory_space=pltpu.HBM)] * 3,
-        out_specs=vmem,
+        out_specs=pl.BlockSpec(memory_space=pltpu.HBM),
         scratch_shapes=[
             pltpu.VMEM(lie.shape, BF16),
             pltpu.VMEM(snap.shape, BF16),
             pltpu.VMEM((modes, rank), F32),
             pltpu.SemaphoreType.DMA((3,)),
+            pltpu.SemaphoreType.DMA((2 * chips * pieces,)),
             pltpu.VMEM((comps, nx, ny * nz, rank), BF16),
             pltpu.VMEM((2, rank // 2, comps * cells), BF16),
             pltpu.VMEM((2, comps, ny * nz, rank), BF16),
@@ -409,7 +417,7 @@
             pltpu.VMEM((2, chips, depth, snaps), F32),
             pltpu.VMEM((extent, 3 * cells), BF16),
             pltpu.VMEM((comps, 2 * chips, modes // (2 * chips), cells), F32),
-            pltpu.VMEM((modes, comps * cells), BF16),
+            pltpu.VMEM((comps * cells, modes), BF16),
             pltpu.VMEM((3, comps, modes, cells), BF16),
             pltpu.VMEM((blocks * 128, comps * cells), BF16),
             pltpu.VMEM((chips, blocks, modes, 128), BF16),
@@ -424,6 +432,8 @@
             collective_id=0, has_side_effects=True, vmem_limit_bytes=60 * 1024 * 1024
         ),
     )(lie, snap, start_block.T)
+    tensor = (tensor.astype(F32) * scale).transpose(1, 0, 2)
+    return tensor.reshape(modes, modes * modes)
 
 
 def solution(mesh):

time: 45.4 us -> 45.1 us (level); the launches traced: 45.3 us -> 44.4 us
  local copies, waits for them, and re-layouts: 2.27 us -> 0 us
  other arithmetic: 0 us -> 2.11 us
  Pallas kernels: 43 us -> 42.3 us
    unnamed x1 -> x0, local copies, waits for them, and re-layouts: 2.27 us -> none
    reshape x0 -> x1, other arithmetic: none -> 2.11 us  [body(): return tensor.reshape(modes, modes * modes)]
    pallas_call x1, Pallas kernels: 43 us -> 42.3 us  [body(): pl.pallas_call(functools.partial(kernel, chips, cols, nz), out_shape=jax....]
where the time goes in v6:
time: 45.1 us; the launch traced here: 44.4 us
  Pallas kernels  42.3 us (94%)
  other arithmetic  2.11 us (5%)
    pallas_call x1, Pallas kernels, body(): pl.pallas_call(functools.partial(kernel, chips, cols, nz), out_shape=jax....  42.3 us
    reshape x1, other arithmetic, body(): return tensor.reshape(modes, modes * modes)  2.11 us

profile of v6, /device:TPU:0, one launch (start us, length us, event | category | flops | bytes accessed | tf_op | source)
XLA Modules:
  0.0 44.4 jit_solution(8505655400583704599)
XLA Ops:
  0.0 42.3 %shard_map.37 = bf16[32,64,128]{2,1,0:T(8,128)(2,1)} custom-call(bf16[64,3,4,128]{3,2,1,0:T(4,128)(2,1)} %bitcast.14, bf16[192,4,512]{2,1,0:T(4,128)(2,1)} %bitcast.13, f32[64,128]{1,0:T(8,128)} %bitcast.15), custom_call_target="tpu_custom_call" | custom-call | tf_op jit(solution)/shard_map/pallas_call | solution.py:397
  42.3 2.1 %copy_bitcast_fusion = f32[64,4096]{1,0:T(8,128)} fusion(bf16[32,64,128]{2,1,0:T(8,128)(2,1)} %shard_map.37), kind=kLoop, calls=%fused_computation | loop fusion | flops 524288 | bytes 1572864 | tf_op jit(solution)/shard_map/reshape | solution.py:436

commit v7 on v6

--- a/solution.py
+++ b/solution.py
@@ -102,14 +102,19 @@
     for c in range(comps):
         sk_ref[c] = lie_ref[:, c].reshape(sk_ref.shape[1:])
 
+    waves = range(sc1.shape[0])
+
     def projection(which):
         half = jnp.dot(sk_cols[which], snaps, preferred_element_type=F32)
-        return half.reshape(sc1.shape)
-
-    sc1[...] = projection(1 - core)
+        size = sc1.shape[-1]
+        return [half[:, w * size:(w + 1) * size].reshape(sc1.shape[1:]) for w in waves]
+
+    for w, value in enumerate(projection(1 - core)):
+        sc1[w] = value
     pl.semaphore_wait(barrier, len(partners))
-    a1 = push(sc1, rc1, a1s.at[0], a1r.at[0], sibling)
-    a1.start()
+    a1 = [push(sc1.at[w], rc1.at[w], a1s.at[w], a1r.at[w], sibling) for w in waves]
+    for copy in a1:
+        copy.start()
     nx, plane = sk_ref.shape[1:3]
     halos = [
         push(sk_ref.at[:, nx - 1], hx.at[0], hs.at[0], hr.at[0], (row_up, col)),
@@ -120,14 +125,18 @@
     for copy in halos:
         copy.start()
     mine = projection(core)
-    a1.wait_recv()
-    acc1[...] = mine + rc1[...]
     a2 = []
-    for o in range(1, chips):
-        q = chip_at(o)
-        copy = push(acc1.at[q], rc2.at[chip], a2s.at[o], a2r.at[chip], on_chip(q))
-        copy.start()
-        a2.append(copy)
+    for w in waves:
+        a1[w].wait_recv()
+        acc1[w] = mine[w] + rc1[w]
+        for o in range(1, chips):
+            q = chip_at(o)
+            copy = push(
+                acc1.at[w, q], rc2.at[w, chip],
+                a2s.at[w * chips + o], a2r.at[w * chips + chip], on_chip(q),
+            )
+            copy.start()
+            a2.append(copy)
 
     extent = diff.shape[0]
     cells = nx * plane
@@ -137,44 +146,56 @@
             jnp.where(place == fore, 0.5, 0.0) - jnp.where(place == aft, 0.5, 0.0)
         ).astype(BF16)
 
-    total = acc1[chip]
-    for o in range(1, chips):
-        q = chip_at(o)
-        push(rc2.at[q], rc2.at[q], a2s.at[o], a2r.at[q], sibling).wait_recv()
-        total = total + rc2[q]
-    rc3[col] = total
     a3 = []
-    for o in range(1, cols):
-        copy = push(rc3.at[col], rc3.at[col], a3s.at[o], a3r.at[col], (row, col_at(o)))
-        copy.start()
-        a3.append(copy)
-    for o in range(1, cols):
-        z = col_at(o)
-        push(rc3.at[z], rc3.at[z], a3s.at[o], a3r.at[z], sibling).wait_recv()
-    total = rc3[0]
-    for z in range(1, cols):
-        total = total + rc3[z]
-    cfull[core, chip] = total
-    own = cfull.at[core, chip]
-    a5 = [push(own, own, a5s.at[0], a5r.at[chip], sibling)]
-    a4 = []
-    for o in range(1, chips):
-        copy = push(own, own, a4s.at[o], a4r.at[chip], on_chip(chip_at(o)))
-        copy.start()
-        a4.append(copy)
-    a5[0].start()
-    for o in range(1, chips):
-        q = chip_at(o)
-        block = cfull.at[core, q]
-        push(block, block, a4s.at[o], a4r.at[q], sibling).wait_recv()
-        copy = push(block, block, a5s.at[o], a5r.at[q], sibling)
+    for w in waves:
+        total = acc1[w, chip]
+        for o in range(1, chips):
+            q = chip_at(o)
+            block = rc2.at[w, q]
+            push(block, block, a2s.at[0], a2r.at[w * chips + q], sibling).wait_recv()
+            total = total + rc2[w, q]
+        rc3[w, col] = total
+        own = rc3.at[w, col]
+        for o in range(1, cols):
+            copy = push(
+                own, own, a3s.at[w * cols + o], a3r.at[w * cols + col], (row, col_at(o))
+            )
+            copy.start()
+            a3.append(copy)
+    a4, a5 = [], []
+    for w in waves:
+        for o in range(1, cols):
+            z = col_at(o)
+            block = rc3.at[w, z]
+            push(block, block, a3s.at[0], a3r.at[w * cols + z], sibling).wait_recv()
+        total = rc3[w, 0]
+        for z in range(1, cols):
+            total = total + rc3[w, z]
+        cfull[w, core, chip] = total
+        own = cfull.at[w, core, chip]
+        for o in range(1, chips):
+            copy = push(
+                own, own, a4s.at[w * chips + o], a4r.at[w * chips + chip], on_chip(chip_at(o))
+            )
+            copy.start()
+            a4.append(copy)
+        copy = push(own, own, a5s.at[w * chips], a5r.at[w * chips + chip], sibling)
         copy.start()
         a5.append(copy)
-    for q in range(chips):
-        block = cfull.at[1 - core, q]
-        push(block, block, a5s.at[0], a5r.at[q], sibling).wait_recv()
-
-    coeffs = cfull[...].reshape(-1, cfull.shape[-1])
+    for w in waves:
+        for o in range(1, chips):
+            q = chip_at(o)
+            block = cfull.at[w, core, q]
+            push(block, block, a4s.at[0], a4r.at[w * chips + q], sibling).wait_recv()
+            copy = push(block, block, a5s.at[w * chips + o], a5r.at[w * chips + q], sibling)
+            copy.start()
+            a5.append(copy)
+    for w in waves:
+        for q in range(chips):
+            block = cfull.at[w, 1 - core, q]
+            push(block, block, a5s.at[0], a5r.at[w * chips + q], sibling).wait_recv()
+
+    coeffs = jnp.concatenate([cfull[w].reshape(rank, -1) for w in waves], axis=1)
     start = start_ref[...]
     modes, rank = start.shape
     coeffs_h, coeffs_l = halves(coeffs)
@@ -370,13 +391,18 @@
 
     for copy in outs:
         copy.wait()
-    for copy in [a1, *halos, *a2, *a3, *a4, *a5, *later]:
+    for copy in [*a1, *halos, *a2, *a3, *a4, *a5, *later]:
         copy.wait_send()
     for q in range(chips):
         push(sg1.at[q], rg1.at[q], g1s.at[q], g1r.at[q], sibling).wait_send()
     for o in range(1, chips):
         q = chip_at(o)
         push(sg2.at[q], rg2.at[q], g2s.at[q], g2r.at[q], sibling).wait_send()
+
+
+def widen(scale, pieces_ref, out_ref):
+    for n in range(pieces_ref.shape[0]):
+        out_ref[:, n * 128:n * 128 + 128] = pieces_ref[n].astype(F32) * scale
 
 
 def body(chips, cols, sketch, snapshots, start_block):
@@ -391,7 +417,9 @@
     blocks = modes * modes // (2 * chips * 128)
     share = max(blocks // cols, 1)
     scale = 1.0 / math.sqrt(cells * 2 * chips * cols)
-    counts = [4, 4, 1, 1] + [chips] * 2 + [cols] * 2 + [chips] * 4
+    waves = 2
+    counts = [4, 4, waves, waves] + [waves * chips] * 2 + [waves * cols] * 2
+    counts += [waves * chips] * 4
     pieces = cols if blocks // cols else 1
     counts += [chips] * 4 + [cols] * 4 + [chips * pieces] * 4
     tensor = pl.pallas_call(
@@ -409,12 +437,12 @@
             pltpu.VMEM((2, rank // 2, comps * cells), BF16),
             pltpu.VMEM((2, comps, ny * nz, rank), BF16),
             pltpu.VMEM((2, comps, nx, 16, rank), BF16),
-            pltpu.VMEM((chips, depth, snaps), F32),
-            pltpu.VMEM((chips, depth, snaps), F32),
-            pltpu.VMEM((chips, depth, snaps), F32),
-            pltpu.VMEM((chips, depth, snaps), F32),
-            pltpu.VMEM((cols, depth, snaps), F32),
-            pltpu.VMEM((2, chips, depth, snaps), F32),
+            pltpu.VMEM((waves, chips, depth, snaps // waves), F32),
+            pltpu.VMEM((waves, chips, depth, snaps // waves), F32),
+            pltpu.VMEM((waves, chips, depth, snaps // waves), F32),
+            pltpu.VMEM((waves, chips, depth, snaps // waves), F32),
+            pltpu.VMEM((waves, cols, depth, snaps // waves), F32),
+            pltpu.VMEM((waves, 2, chips, depth, snaps // waves), F32),
             pltpu.VMEM((extent, 3 * cells), BF16),
             pltpu.VMEM((comps, 2 * chips, modes // (2 * chips), cells), F32),
             pltpu.VMEM((comps * cells, modes), BF16),
@@ -432,8 +460,14 @@
             collective_id=0, has_side_effects=True, vmem_limit_bytes=60 * 1024 * 1024
         ),
     )(lie, snap, start_block.T)
-    tensor = (tensor.astype(F32) * scale).transpose(1, 0, 2)
-    return tensor.reshape(modes, modes * modes)
+    step = 8
+    return pl.pallas_call(
+        functools.partial(widen, scale),
+        grid=(2 * chips * blocks // step,),
+        out_shape=jax.ShapeDtypeStruct((modes, modes * modes), F32),
+        in_specs=[pl.BlockSpec((step, modes, 128), lambda n: (n, 0, 0))],
+        out_specs=pl.BlockSpec((modes, step * 128), lambda n: (0, n)),
+    )(tensor)
 
 
 def solution(mesh):

time: 45.1 us -> 46.1 us (1.022)
  Pallas kernels: 42.3 us -> 45.3 us
  other arithmetic: 2.11 us -> 0 us
    pallas_call x0 -> x1, Pallas kernels: none -> 3.28 us  [body(): pl.pallas_call(functools.partial(widen, scale), grid=(2 * chips * blocks...]
    reshape x1 -> x0, other arithmetic: 2.11 us -> none  [body(): return tensor.reshape(modes, modes * modes)]
where the time goes in v7:
time: 46.1 us; the launch traced here: 45.3 us
  Pallas kernels  45.3 us (98%)
    pallas_call x1, Pallas kernels, body(): pl.pallas_call(functools.partial(kernel, chips, cols, nz), out_shape=jax....  42 us
    pallas_call x1, Pallas kernels, body(): pl.pallas_call(functools.partial(widen, scale), grid=(2 * chips * blocks...  3.28 us

profile of v7, /device:TPU:0, one launch (start us, length us, event | category | flops | bytes accessed | tf_op | source)
XLA Modules:
  0.0 45.3 jit_solution(16128813708396164433)
XLA Ops:
  0.0 42.0 %shard_map.37.pieces_ref = bf16[32,64,128]{2,1,0:T(8,128)(2,1)} custom-call(bf16[64,3,4,128]{3,2,1,0:T(4,128)(2,1)} %bitcast.8, bf16[192,4,512]{2,1,0:T(4,128)(2,1)} %bitcast.7, f32[64,128]{1,0:T(8,128)} %bitcast.9), custom_call_target="tpu_custom_call" | custom-call | tf_op jit(solution)/shard_map/pallas_call | solution.py:425
  42.0 3.3 %shard_map.38 = f32[64,4096]{1,0:T(8,128)} custom-call(bf16[32,64,128]{2,1,0:T(8,128)(2,1)} %shard_map.37.pieces_ref), custom_call_target="tpu_custom_call" | custom-call | tf_op jit(solution)/shard_map/pallas_call | solution.py:464

commit v8 on v7

--- a/solution.py
+++ b/solution.py
@@ -347,12 +347,15 @@
     outs = []
 
     def write(which, q, z):
-        slot = (which * chips + q) * pieces + z
-        copy = pltpu.make_async_copy(
-            piece(which, q, z), out_ref.at[pl.ds(slot * width, width)], stores.at[slot]
-        )
-        copy.start()
-        outs.append(copy)
+        for n in range(width):
+            block = z * width + n
+            slot = (which * chips + q) * blocks + block
+            lanes = pl.ds(pl.multiple_of(slot * 128, 128), 128)
+            copy = pltpu.make_async_copy(
+                gfull.at[which, q, block], out_ref.at[:, lanes], stores.at[slot]
+            )
+            copy.start()
+            outs.append(copy)
 
     def forward(q, z):
         part_of = piece(core, q, z)
@@ -398,11 +401,6 @@
     for o in range(1, chips):
         q = chip_at(o)
         push(sg2.at[q], rg2.at[q], g2s.at[q], g2r.at[q], sibling).wait_send()
-
-
-def widen(scale, pieces_ref, out_ref):
-    for n in range(pieces_ref.shape[0]):
-        out_ref[:, n * 128:n * 128 + 128] = pieces_ref[n].astype(F32) * scale
 
 
 def body(chips, cols, sketch, snapshots, start_block):
@@ -424,7 +422,7 @@
     counts += [chips] * 4 + [cols] * 4 + [chips * pieces] * 4
     tensor = pl.pallas_call(
         functools.partial(kernel, chips, cols, nz),
-        out_shape=jax.ShapeDtypeStruct((2 * chips * blocks, modes, 128), BF16),
+        out_shape=jax.ShapeDtypeStruct((modes, modes * modes), BF16),
         in_specs=[pl.BlockSpec(memory_space=pltpu.HBM)] * 3,
         out_specs=pl.BlockSpec(memory_space=pltpu.HBM),
         scratch_shapes=[
@@ -432,7 +430,7 @@
             pltpu.VMEM(snap.shape, BF16),
             pltpu.VMEM((modes, rank), F32),
             pltpu.SemaphoreType.DMA((3,)),
-            pltpu.SemaphoreType.DMA((2 * chips * pieces,)),
+            pltpu.SemaphoreType.DMA((2 * chips * blocks,)),
             pltpu.VMEM((comps, nx, ny * nz, rank), BF16),
             pltpu.VMEM((2, rank // 2, comps * cells), BF16),
             pltpu.VMEM((2, comps, ny * nz, rank), BF16),
@@ -460,14 +458,7 @@
             collective_id=0, has_side_effects=True, vmem_limit_bytes=60 * 1024 * 1024
         ),
     )(lie, snap, start_block.T)
-    step = 8
-    return pl.pallas_call(
-        functools.partial(widen, scale),
-        grid=(2 * chips * blocks // step,),
-        out_shape=jax.ShapeDtypeStruct((modes, modes * modes), F32),
-        in_specs=[pl.BlockSpec((step, modes, 128), lambda n: (n, 0, 0))],
-        out_specs=pl.BlockSpec((modes, step * 128), lambda n: (0, n)),
-    )(tensor)
+    return tensor.astype(F32) * scale
 
 
 def solution(mesh):

time: 46.1 us -> 44.9 us (0.974)
  Pallas kernels: 45.3 us -> 42 us
  other arithmetic: 0 us -> 2.1 us
    pallas_call x1 -> x0, Pallas kernels: 3.28 us -> none  [body(): pl.pallas_call(functools.partial(widen, scale), grid=(2 * chips * blocks...]
    mul x0 -> x1, other arithmetic: none -> 2.1 us  [body(): return tensor.astype(F32) * scale]
where the time goes in v8:
time: 44.9 us; the launch traced here: 44.2 us
  Pallas kernels  42 us (94%)
  other arithmetic  2.1 us (5%)
    pallas_call x1, Pallas kernels, body(): pl.pallas_call(functools.partial(kernel, chips, cols, nz), out_shape=jax....  42 us
    mul x1, other arithmetic, body(): return tensor.astype(F32) * scale  2.1 us

profile of v8, /device:TPU:0, one launch (start us, length us, event | category | flops | bytes accessed | tf_op | source)
XLA Modules:
  0.0 44.2 jit_solution(3493332055844106598)
XLA Ops:
  0.0 42.0 %shard_map.37 = bf16[64,4096]{1,0:T(8,128)(2,1)} custom-call(bf16[64,3,4,128]{3,2,1,0:T(4,128)(2,1)} %bitcast.8, bf16[192,4,512]{2,1,0:T(4,128)(2,1)} %bitcast.7, f32[64,128]{1,0:T(8,128)} %bitcast.9), custom_call_target="tpu_custom_call" | custom-call | tf_op jit(solution)/shard_map/pallas_call | solution.py:423
  42.0 2.1 %convert_multiply_fusion = f32[64,4096]{1,0:T(8,128)} fusion(bf16[64,4096]{1,0:T(8,128)(2,1)} %shard_map.37), kind=kLoop, calls=%fused_computation | loop fusion | flops 524288 | bytes 1572864 | tf_op jit(solution)/shard_map/mul | solution.py:461

commit v9 on v8

--- a/solution.py
+++ b/solution.py
@@ -53,7 +53,7 @@
     lie_ref, snap_ref, start_ref, loads, stores, sk_ref, sk_cols, hx, hy, sc1, rc1, acc1, rc2, rc3, cfull,
     diff, phi, phi_all, grad, adv,
     sg1, rg1, sg2, rg2, sg3, rg3, gfull,
-    hs, hr, a1s, a1r, a2s, a2r, a3s, a3r, a4s, a4r, a5s, a5r,
+    hs, hr, a1s, a1r, a2s, a2r, a3s, a3r, a4s, a4r,
     g1s, g1r, g2s, g2r, g3s, g3r, g4s, g4r, g5s, g5r, g6s, g6r,
 ):
     rows = 2 * chips
@@ -62,7 +62,6 @@
     sibling = (row + 1 - 2 * core, col)
     row_up, row_down = lax.rem(row + 1, rows), lax.rem(row + rows - 1, rows)
     col_up, col_down = lax.rem(col + 1, cols), lax.rem(col + cols - 1, cols)
-    row_other = lax.rem(row + rows + 2 * core - 1, rows)
 
     def chip_at(offset):
         return lax.rem(chip + offset, chips)
@@ -88,8 +87,7 @@
     for copy in fetches:
         copy.start()
     barrier = pltpu.get_barrier_semaphore()
-    partners = [sibling, (row_other, col)]
-    partners += [on_chip(chip_at(o)) for o in range(1, chips)]
+    partners = [(lax.rem(row + o, rows), col) for o in range(1, rows)]
     partners += [(row, col_at(o)) for o in range(1, cols)]
     for device in partners:
         pl.semaphore_signal(barrier, inc=1, device_id=device, device_id_type=MESH)
@@ -162,7 +160,7 @@
             )
             copy.start()
             a3.append(copy)
-    a4, a5 = [], []
+    a4 = []
     for w in waves:
         for o in range(1, cols):
             z = col_at(o)
@@ -173,27 +171,18 @@
             total = total + rc3[w, z]
         cfull[w, core, chip] = total
         own = cfull.at[w, core, chip]
-        for o in range(1, chips):
+        for o in range(1, rows):
             copy = push(
-                own, own, a4s.at[w * chips + o], a4r.at[w * chips + chip], on_chip(chip_at(o))
+                own, own, a4s.at[w * rows + o], a4r.at[w * rows + row],
+                (lax.rem(row + o, rows), col),
             )
             copy.start()
             a4.append(copy)
-        copy = push(own, own, a5s.at[w * chips], a5r.at[w * chips + chip], sibling)
-        copy.start()
-        a5.append(copy)
     for w in waves:
-        for o in range(1, chips):
-            q = chip_at(o)
-            block = cfull.at[w, core, q]
-            push(block, block, a4s.at[0], a4r.at[w * chips + q], sibling).wait_recv()
-            copy = push(block, block, a5s.at[w * chips + o], a5r.at[w * chips + q], sibling)
-            copy.start()
-            a5.append(copy)
-    for w in waves:
-        for q in range(chips):
-            block = cfull.at[w, 1 - core, q]
-            push(block, block, a5s.at[0], a5r.at[w * chips + q], sibling).wait_recv()
+        for o in range(1, rows):
+            r = lax.rem(row + o, rows)
+            block = cfull.at[w, lax.rem(r, 2), r // 2]
+            push(block, block, a4s.at[0], a4r.at[w * rows + r], sibling).wait_recv()
 
     coeffs = jnp.concatenate([cfull[w].reshape(rank, -1) for w in waves], axis=1)
     start = start_ref[...]
@@ -394,7 +383,7 @@
 
     for copy in outs:
         copy.wait()
-    for copy in [*a1, *halos, *a2, *a3, *a4, *a5, *later]:
+    for copy in [*a1, *halos, *a2, *a3, *a4, *later]:
         copy.wait_send()
     for q in range(chips):
         push(sg1.at[q], rg1.at[q], g1s.at[q], g1r.at[q], sibling).wait_send()
@@ -417,7 +406,7 @@
     scale = 1.0 / math.sqrt(cells * 2 * chips * cols)
     waves = 2
     counts = [4, 4, waves, waves] + [waves * chips] * 2 + [waves * cols] * 2
-    counts += [waves * chips] * 4
+    counts += [waves * 2 * chips] * 2
     pieces = cols if blocks // cols else 1
     counts += [chips] * 4 + [cols] * 4 + [chips * pieces] * 4
     tensor = pl.pallas_call(

time: 44.9 us -> 44.9 us (level)
  no operation moved by 1% of the time
where the time goes in v9:
time: 44.9 us; the launch traced here: 44.1 us
  Pallas kernels  42 us (94%)
  other arithmetic  2.1 us (5%)
    pallas_call x1, Pallas kernels, body(): pl.pallas_call(functools.partial(kernel, chips, cols, nz), out_shape=jax....  42 us
    mul x1, other arithmetic, body(): return tensor.astype(F32) * scale  2.1 us

profile of v9, /device:TPU:0, one launch (start us, length us, event | category | flops | bytes accessed | tf_op | source)
XLA Modules:
  0.0 44.1 jit_solution(3395113012776679883)
XLA Ops:
  0.0 42.0 %shard_map.37 = bf16[64,4096]{1,0:T(8,128)(2,1)} custom-call(bf16[64,3,4,128]{3,2,1,0:T(4,128)(2,1)} %bitcast.8, bf16[192,4,512]{2,1,0:T(4,128)(2,1)} %bitcast.7, f32[64,128]{1,0:T(8,128)} %bitcast.9), custom_call_target="tpu_custom_call" | custom-call | tf_op jit(solution)/shard_map/pallas_call | solution.py:412
  42.0 2.1 %convert_multiply_fusion = f32[64,4096]{1,0:T(8,128)} fusion(bf16[64,4096]{1,0:T(8,128)(2,1)} %shard_map.37), kind=kLoop, calls=%fused_computation | loop fusion | flops 524288 | bytes 1572864 | tf_op jit(solution)/shard_map/mul | solution.py:450

commit v10 on v8

--- a/solution.py
+++ b/solution.py
@@ -82,7 +82,7 @@
     fetches = [
         pltpu.make_async_copy(src, dst, loads.at[n])
         for n, (src, dst) in enumerate(
-            [(snap_hbm, snap_ref), (lie_hbm, lie_ref), (start_hbm, start_ref)]
+            [(lie_hbm, lie_ref), (snap_hbm, snap_ref), (start_hbm, start_ref)]
         )
     ]
     for copy in fetches:
@@ -95,12 +95,10 @@
         pl.semaphore_signal(barrier, inc=1, device_id=device, device_id_type=MESH)
 
     comps, rank = sk_ref.shape[0], sk_ref.shape[-1]
-    for copy in fetches:
-        copy.wait()
+    fetches[0].wait()
+    sk_cols[...] = lie_ref[...].reshape(-1, rank).T.reshape(sk_cols.shape)
+    fetches[1].wait()
     snaps = snap_ref[...].reshape(-1, snap_ref.shape[-1])
-    sk_cols[...] = lie_ref[...].reshape(-1, rank).T.reshape(sk_cols.shape)
-    for c in range(comps):
-        sk_ref[c] = lie_ref[:, c].reshape(sk_ref.shape[1:])
 
     waves = range(sc1.shape[0])
 
@@ -115,6 +113,9 @@
     a1 = [push(sc1.at[w], rc1.at[w], a1s.at[w], a1r.at[w], sibling) for w in waves]
     for copy in a1:
         copy.start()
+    mine = projection(core)
+    for c in range(comps):
+        sk_ref[c] = lie_ref[:, c].reshape(sk_ref.shape[1:])
     nx, plane = sk_ref.shape[1:3]
     halos = [
         push(sk_ref.at[:, nx - 1], hx.at[0], hs.at[0], hr.at[0], (row_up, col)),
@@ -122,9 +123,6 @@
         push(sk_ref.at[:, :, pl.ds(plane - 16, 16)], hy.at[0], hs.at[2], hr.at[2], (row, col_up)),
         push(sk_ref.at[:, :, pl.ds(0, 16)], hy.at[1], hs.at[3], hr.at[3], (row, col_down)),
     ]
-    for copy in halos:
-        copy.start()
-    mine = projection(core)
     a2 = []
     for w in waves:
         a1[w].wait_recv()
@@ -137,6 +135,8 @@
             )
             copy.start()
             a2.append(copy)
+    for copy in halos:
+        copy.start()
 
     extent = diff.shape[0]
     cells = nx * plane
@@ -196,6 +196,7 @@
             push(block, block, a5s.at[0], a5r.at[w * chips + q], sibling).wait_recv()
 
     coeffs = jnp.concatenate([cfull[w].reshape(rank, -1) for w in waves], axis=1)
+    fetches[2].wait()
     start = start_ref[...]
     modes, rank = start.shape
     coeffs_h, coeffs_l = halves(coeffs)

time: 44.9 us -> 44.8 us (level)
  no operation moved by 1% of the time
where the time goes in v10:
time: 44.8 us; the launch traced here: 44 us
  Pallas kernels  41.9 us (94%)
  other arithmetic  2.1 us (5%)
    pallas_call x1, Pallas kernels, body(): pl.pallas_call(functools.partial(kernel, chips, cols, nz), out_shape=jax....  41.9 us
    mul x1, other arithmetic, body(): return tensor.astype(F32) * scale  2.1 us

profile of v10, /device:TPU:0, one launch (start us, length us, event | category | flops | bytes accessed | tf_op | source)
XLA Modules:
  0.0 44.0 jit_solution(2532422109526442532)
XLA Ops:
  0.0 41.9 %shard_map.37 = bf16[64,4096]{1,0:T(8,128)(2,1)} custom-call(bf16[64,3,4,128]{3,2,1,0:T(4,128)(2,1)} %bitcast.8, bf16[192,4,512]{2,1,0:T(4,128)(2,1)} %bitcast.7, f32[64,128]{1,0:T(8,128)} %bitcast.9), custom_call_target="tpu_custom_call" | custom-call | tf_op jit(solution)/shard_map/pallas_call | solution.py:424
  41.9 2.1 %convert_multiply_fusion = f32[64,4096]{1,0:T(8,128)} fusion(bf16[64,4096]{1,0:T(8,128)(2,1)} %shard_map.37), kind=kLoop, calls=%fused_computation | loop fusion | flops 524288 | bytes 1572864 | tf_op jit(solution)/shard_map/mul | solution.py:462
